TPU v7x, 32 devices: a whole 2x2x4 slice. The times are simulated.
32 devices in a mesh: comp: 8 (over z, y), rank: 4 (over x, core).
Axes of the slice: x: 2, y: 2, z: 4, core: 2. Of those that a mesh axis runs over, the one named last changes fastest.
Arguments:
- density: float32 [32, 16384], P('comp'), may hold values from 0.1 to 1
- row_left: float32 [8, 32], replicated, may hold values from -4 to 4
- col_left: float32 [8, 16384], replicated, may hold values from -4 to 4
- row_right: float32 [8, 32], replicated, may hold values from -4 to 4
- col_right: float32 [8, 16384], replicated, may hold values from -4 to 4
Outputs:
- gain: float32 [32, 16384], P(('comp', 'rank'))
All inputs are finite; a program needn't handle non-finite values.
Results may differ from a plain program's by a relative error of at most 0.00021.
Values sent between devices are 32-bit elements; how exact they have to be, the bound alone decides.
No kernel may reach another device: no remote copies, remote signals or barrier semaphores. Data moves between devices by JAX's collectives and lax.ppermute only.
A program may use at most 192 MiB of HBM per device.

v0:
```python
import math

import jax
import jax.numpy as jnp
import numpy as np
from jax import lax
from jax.experimental import pallas as pl
from jax.experimental.pallas import tpu as pltpu
from jax.sharding import PartitionSpec as P

LANES = 128
VMEM_BYTES = 16 * 1024 * 1024
AXES = ("comp", "rank")
PAD = 4
HELD_PARTS = (0, 2, 1, 3)


def split_parts(values):
    high = values.astype(jnp.bfloat16)
    low = (values - high.astype(jnp.float32)).astype(jnp.bfloat16)
    return high, low


def split_rows(table):
    high, low = split_parts(jnp.asarray(table, jnp.float32))
    return jnp.concatenate([high, high, low], axis=0)


def split_columns(table):
    high, low = split_parts(jnp.asarray(table, jnp.float32))
    return jnp.concatenate([high, high, low], axis=1)


def dot_split(rows, table):
    high, low = split_parts(rows)
    joined = jnp.concatenate([high, low, high], axis=1)
    return jnp.dot(joined, table, preferred_element_type=jnp.float32)


def forward_table():
    angles = 2.0 * np.pi * np.outer(np.arange(LANES), np.arange(LANES)) / LANES
    cosine, sine = np.cos(angles), np.sin(angles)
    return np.block([[cosine, -sine], [sine, cosine]])


def inverse_table():
    angles = 2.0 * np.pi * np.outer(np.arange(LANES), np.arange(LANES)) / LANES
    return np.concatenate([np.cos(angles), -np.sin(angles)], axis=0)


def block_twiddles(blocks):
    angles = 2.0 * np.pi * np.outer(np.arange(blocks), np.arange(LANES)) / (blocks * LANES)
    table = np.stack([np.cos(angles), -np.sin(angles)], axis=1)
    return jnp.asarray(
        np.broadcast_to(table[:, :, None, :], (blocks, 2, 8, LANES)), jnp.float32
    )


def final_tables(devices, groups, blocks, width):
    owner = np.arange(devices) % groups
    frequency = (owner[:, None] + groups * np.arange(blocks)[None, :]).astype(np.float64) + 0.25
    frequency = np.broadcast_to(frequency[:, None, :], (devices, 2, blocks))
    inner = 2.0 * np.pi * frequency[..., None] * np.arange(LANES) / width
    rows = devices * 2 * blocks
    inner_cos = np.cos(inner).reshape(rows, LANES)
    inner_sin = np.sin(inner).reshape(rows, LANES)
    outer_count = width // LANES
    outer = 2.0 * np.pi * frequency * LANES / width
    outer = np.arange(outer_count)[:, None] * outer.reshape(1, rows)
    is_real = np.broadcast_to(np.array([True, False])[None, :, None], (devices, 2, blocks))
    is_real = is_real.reshape(1, rows)
    with_cos = np.where(is_real, np.cos(outer), -np.sin(outer))
    with_sin = np.where(is_real, -np.sin(outer), -np.cos(outer))
    return inner_cos, inner_sin, np.concatenate([with_cos, with_sin], axis=1)


def block_fourier(reals, imags):
    count = len(reals)
    if count == 1:
        return reals, imags
    if count == 2:
        return (
            [reals[0] + reals[1], reals[0] - reals[1]],
            [imags[0] + imags[1], imags[0] - imags[1]],
        )
    even_real, odd_real = reals[0] + reals[2], reals[0] - reals[2]
    even_imag, odd_imag = imags[0] + imags[2], imags[0] - imags[2]
    pair_real, gap_real = reals[1] + reals[3], reals[1] - reals[3]
    pair_imag, gap_imag = imags[1] + imags[3], imags[1] - imags[3]
    return (
        [even_real + pair_real, odd_real + gap_imag, even_real - pair_real, odd_real - gap_imag],
        [even_imag + pair_imag, odd_imag - gap_real, even_imag - pair_imag, odd_imag + gap_real],
    )


def reduce_rows(blocks, rows, terms, fetch, factors_at, starts, span, partial):
    inner = blocks * LANES
    outer = span // inner
    unroll = math.gcd(16, outer)

    def reduce_block(block, first, count):
        sums = (jnp.zeros((terms, LANES), jnp.float32),) * (4 * count)
        for part, start in enumerate(starts):

            def step(at, sums, part=part, start=start):
                sums = list(sums)
                for extra in range(unroll):
                    lane = (at * unroll + extra) * inner + block * LANES
                    factors = factors_at(start + lane, first == 0)
                    for row in range(count):
                        value = fetch(part, first + row, lane)
                        value = jnp.broadcast_to(value, (terms, LANES))
                        for k in range(4):
                            sums[row * 4 + k] += value * factors[k]
                return tuple(sums)

            sums = lax.fori_loop(0, outer // unroll, step, sums)
        for row in range(count):
            for k in range(4):
                partial[k, block, first + row] = sums[row * 4 + k]

    def reduce_tiles(block, carry):
        for first in range(0, rows, 8):
            reduce_block(block, first, min(8, rows - first))
        return carry

    lax.fori_loop(0, blocks, reduce_tiles, 0)


def transform_rows(blocks, rows, row_at, row_factors, twiddle, table, out, partial, joined):
    terms, total_rows = row_factors[0].shape
    lanes = lax.broadcasted_iota(jnp.int32, (terms, total_rows), 1)

    def butterfly(row, side):
        picked = jnp.where(lanes == row_at(row), row_factors[side][...], 0.0)
        factor = jnp.sum(picked, axis=1, keepdims=True)
        factor = jnp.broadcast_to(factor, (terms, LANES))
        reals = [partial[2 * side, block, row] * factor for block in range(blocks)]
        imags = [partial[2 * side + 1, block, row] * factor for block in range(blocks)]
        reals, imags = block_fourier(reals, imags)
        for block in range(1, blocks):
            real, imag = reals[block], imags[block]
            cosine, sine = twiddle[block, 0], twiddle[block, 1]
            reals[block] = real * cosine - imag * sine
            imags[block] = real * sine + imag * cosine
        return reals, imags

    def butterfly_pair(pair):
        for side in range(2):
            both = [butterfly(pair * 2 + extra, side) for extra in range(2)]
            for block in range(blocks):
                base = ((block * 2 + side) * rows + pair * 2) * terms
                place = pl.ds(base, 2 * terms)
                for part in range(2):
                    values = jnp.concatenate([both[0][part][block], both[1][part][block]], axis=0)
                    high, low = split_parts(values)
                    for third, piece in enumerate((high, low, high)):
                        joined[place, pl.ds((third * 2 + part) * LANES, LANES)] = piece

    for pair in range(rows // 2):
        butterfly_pair(pair)
    planes = 2 * blocks
    step = planes * rows * terms
    while step > 512:
        step //= 2
    plane_step = step // (rows * terms)

    def transform(at, carry):
        place = pl.ds(pl.multiple_of(at * step, 16), step)
        total = jnp.dot(joined[place, :], table[...], preferred_element_type=jnp.float32)
        total = total.reshape(plane_step, rows, terms, 2 * LANES)
        place = pl.ds(at * plane_step, plane_step)
        out[place, 0] = total[..., :LANES]
        out[place, 1] = total[..., LANES:]
        return carry

    lax.fori_loop(0, planes // plane_step, transform, 0)


def comp_of(step, flipped):
    lines = lax.axis_size("comp") // 2
    comp_at = lax.axis_index("comp")
    line = lax.rem(lax.div(comp_at, 2) + lines - step, lines)
    side = lax.rem(comp_at, 2)
    return line * 2 + (1 - side if flipped else side)


def make_phases(groups, phases):
    width = phases.shape[1] * LANES
    device_at = lax.axis_index("comp") * lax.axis_size("rank") + lax.axis_index("rank")
    odd = 4 * lax.rem(device_at, groups) + 1
    shape = phases.shape[1:]
    cells = lax.broadcasted_iota(jnp.int32, shape, 0) * LANES
    cells = cells + lax.broadcasted_iota(jnp.int32, shape, 1)
    turns = (cells * odd) & (4 * width - 1)
    turns = jnp.where(turns >= 2 * width, turns - 4 * width, turns)
    angles = turns.astype(jnp.float32) * (2.0 * math.pi / (4 * width))
    phases[0] = jnp.cos(angles)
    phases[1] = -jnp.sin(angles)


def made_factors(columns, phases, kept):
    terms = columns[0].shape[0]

    def factors_at(lane, first):
        place = pl.ds(pl.multiple_of(lane, LANES), LANES)
        if not first:
            return [kept[k, :, place] for k in range(4)]
        turn = pl.ds(lax.div(lane, LANES), 1)
        factors = [
            column[:, place] * jnp.broadcast_to(phases[part, turn, :], (terms, LANES))
            for column in columns
            for part in range(2)
        ]
        for k in range(4):
            kept[k, :, place] = factors[k]
        return factors

    return factors_at


def start_tables(tables, held, arrivals):
    copies = [
        pltpu.make_async_copy(table, place, arrivals.at[k])
        for k, (table, place) in enumerate(zip(tables, held))
    ]
    for copy in copies:
        copy.start()
    return copies


def pieces_kernel(blocks, groups, sources, count, *refs):
    pieces, refs = refs[:count], refs[count:]
    columns, row_factors, tables, refs = refs[0:2], refs[2:4], refs[4:6], refs[6:]
    out, partial, joined, phases, weights, twiddle, table, arrivals = refs
    copies = start_tables(tables, (twiddle, table), arrivals)
    make_phases(groups, phases)
    reduce_pieces(blocks, sources, pieces, columns, phases, weights, partial)
    finish_pieces(
        blocks, sources, copies, row_factors, twiddle, table, out, partial, joined
    )


def own_kernel(blocks, groups, sources, *refs):
    row_factors, sent, refs = refs[0:2], refs[2:7], refs[7:]
    out, partial, joined, phases, weights = refs[:5]
    held, arrivals = refs[5:10], refs[10]
    copies = start_tables(sent, held, arrivals)
    make_phases(groups, phases)
    for copy in copies[2:]:
        copy.wait()
    twiddle, table, own, *columns = held
    reduce_pieces(blocks, sources, [own], columns, phases, weights, partial)
    finish_pieces(
        blocks, sources, copies[:2], row_factors, twiddle, table, out, partial, joined
    )


def reduce_pieces(blocks, sources, pieces, columns, phases, weights, partial):
    rows_here = pieces[0].shape[-2]
    terms, width = columns[0].shape
    ranks = lax.axis_size("rank")
    span = width // ranks
    rank_at = lax.axis_index("rank")
    starts = [(rank_at ^ other) * span for other in HELD_PARTS]

    def fetch(part, row, lane):
        quarters, _, _ = sources[row // rows_here]
        row = pl.ds(row % rows_here, 1)
        if quarters is None:
            return pieces[0][row, pl.ds(pl.multiple_of(starts[part] + lane, LANES), LANES)]
        number, index = quarters[part]
        return pieces[number][index, row, pl.ds(pl.multiple_of(lane, LANES), LANES)]

    factors_at = made_factors(columns, phases, weights)
    rows = len(sources) * rows_here
    reduce_rows(blocks, rows, terms, fetch, factors_at, starts, span, partial)


def finish_pieces(blocks, sources, copies, row_factors, twiddle, table, out, partial, joined):
    rows = partial.shape[2]
    rows_here = rows // len(sources)
    bases = [comp_of(step, flipped) * rows_here for _, step, flipped in sources]

    def row_at(row):
        return bases[row // rows_here] + row % rows_here

    for copy in copies:
        copy.wait()
    transform_rows(blocks, rows, row_at, row_factors, twiddle, table, out, partial, joined)


def gathered_kernel(blocks, groups, pieces, *refs):
    columns, row_factors, tables, refs = refs[0:2], refs[2:4], refs[4:6], refs[6:]
    out, partial, joined, phases, weights, twiddle, table, arrivals = refs
    copies = start_tables(tables, (twiddle, table), arrivals)
    make_phases(groups, phases)
    parts, rows_here, span = pieces.shape[1:]

    def fetch(part, row, lane):
        place = pl.ds(pl.multiple_of(lane, LANES), LANES)
        return pieces[row // rows_here, part, pl.ds(row % rows_here, 1), place]

    base = pl.program_id(0) * 8
    starts = [part * span for part in range(parts)]
    terms = columns[0].shape[0]
    factors_at = made_factors(columns, phases, weights)
    reduce_rows(blocks, 8, terms, fetch, factors_at, starts, span, partial)
    for copy in copies:
        copy.wait()
    transform_rows(
        blocks,
        8,
        lambda row: base + row,
        row_factors,
        twiddle,
        table,
        out.at[0],
        partial,
        joined,
    )


def pass_kernel(*refs):
    del refs


def after(values, earlier):
    anywhere = pl.BlockSpec(memory_space=pl.ANY)
    operands = [pltpu.with_memory_space_constraint(x, pltpu.VMEM) for x in (*values, earlier)]
    return pl.pallas_call(
        pass_kernel,
        out_shape=[jax.ShapeDtypeStruct(value.shape, value.dtype) for value in values],
        in_specs=[anywhere] * len(operands),
        out_specs=[anywhere] * len(values),
        input_output_aliases={k: k for k in range(len(values))},
    )(*operands)


def convolve_kernel(blocks, rows_here, layout, tile_count, *refs):
    tiles = refs[:tile_count]
    back, out, spectrum, product, mixed = refs[tile_count:]
    total_rows = spectrum.shape[2] - PAD
    terms = spectrum.shape[3]
    spectrum[:, :, pl.ds(0, PAD)] = jnp.zeros((2 * blocks, 3, PAD, terms, LANES), jnp.float32)
    moves = []
    for number, tile in enumerate(tiles):
        for at in range(tile.shape[0]):
            for first in range(0, tile.shape[3], rows_here):
                moves.append((tile, at, first))
    comps = [comp_of(*layout[k]) if layout else k for k in range(len(moves))]

    def collect(plane, carry):
        for (tile, at, first), comp in zip(moves, comps):
            real = tile[at, plane, 0, pl.ds(first, rows_here)]
            imag = tile[at, plane, 1, pl.ds(first, rows_here)]
            place = pl.ds(PAD + comp * rows_here, rows_here)
            spectrum[plane, 0, place] = real
            spectrum[plane, 1, place] = imag
            spectrum[plane, 2, place] = real + imag
        return carry

    lax.fori_loop(0, 2 * blocks, collect, 0)

    def step(at, sums, block, out_tile, whole):
        sums = list(sums)
        left_base = PAD + 4 * at
        right_base = PAD + 4 * (out_tile - at)
        for part in range(3):
            left = [spectrum[2 * block, part, left_base + k] for k in range(4)]
            right = {
                k: spectrum[2 * block + 1, part, right_base + k]
                for k in range(-3 if whole else 0, 4)
            }
            for row in range(4):
                for k in range(4 if whole else row + 1):
                    sums[row * 3 + part] += left[k] * right[row - k]
        return tuple(sums)

    def finish(sums, block, out_tile):
        for row in range(4):
            both_real, both_imag, crossed = sums[row * 3 : row * 3 + 3]
            base = (out_tile * 4 + row) * 2 * blocks + block
            product[base] = both_real - both_imag
            product[base + blocks] = crossed - both_real - both_imag

    zeros = (jnp.zeros((terms, LANES), jnp.float32),) * 12
    out_tiles = total_rows // 4

    def convolve_block(block, carry):
        for out_tile in range(out_tiles):
            sums = zeros
            for at in range(out_tile + 1):
                sums = step(at, sums, block, out_tile, at < out_tile)
            finish(sums, block, out_tile)
        return carry

    def convolve_tile(index, carry):
        block = lax.rem(index, blocks)
        out_tile = lax.div(index, blocks)
        sums = lax.fori_loop(
            0, out_tile + 1, lambda at, sums: step(at, sums, block, out_tile, True), zeros
        )
        finish(sums, block, out_tile)
        return carry

    if total_rows <= 32:
        lax.fori_loop(0, blocks, convolve_block, 0)
    else:
        lax.fori_loop(0, out_tiles * blocks, convolve_tile, 0)

    def gather_terms(at, carry):
        tiles = [product[at * 8 + k] for k in range(8)]
        summed = jnp.sum(jnp.stack(tiles), axis=1)
        if blocks == 4:
            turned = jnp.concatenate([summed[blocks:], -summed[:blocks]], axis=0)
        else:
            swapped = [
                tiles[k + blocks] if (k // blocks) % 2 == 0 else -tiles[k - blocks]
                for k in range(8)
            ]
            turned = jnp.sum(jnp.stack(swapped), axis=1)
        place = pl.ds(pl.multiple_of(at * 8, 8), 8)
        mixed[place, pl.ds(0, LANES)] = summed
        mixed[place, pl.ds(LANES, LANES)] = turned
        return carry

    lax.fori_loop(0, total_rows * 2 * blocks // 8, gather_terms, 0, unroll=4)
    out[...] = dot_split(mixed[...], back[...])


def final_kernel(scaling, spread, inner_cos, inner_sin, outer, out):
    values = spread[...]
    stacked = jnp.concatenate([values * inner_cos[...], values * inner_sin[...]], axis=0)
    high, low = split_parts(stacked)
    joined = jnp.concatenate([high, low, high], axis=0)
    total = jnp.dot(outer[...], joined, preferred_element_type=jnp.float32)
    out[...] = total * scaling


def in_hbm(array):
    return pltpu.with_memory_space_constraint(array, pltpu.HBM)


def whole_call(kernel, out_shapes, scratch, operands, tables=(), kept=True):
    out_type = pltpu.VMEM if kept else jax.ShapeDtypeStruct
    operands = [pltpu.with_memory_space_constraint(operand, pltpu.VMEM) for operand in operands]
    return pl.pallas_call(
        kernel,
        out_shape=[out_type(shape, jnp.float32) for shape in out_shapes],
        in_specs=[pl.BlockSpec(memory_space=pltpu.VMEM)] * len(operands)
        + [pl.BlockSpec(memory_space=pltpu.HBM)] * len(tables),
        out_specs=[pl.BlockSpec(memory_space=pltpu.VMEM)] * len(out_shapes),
        scratch_shapes=scratch,
        compiler_params=pltpu.CompilerParams(vmem_limit_bytes=VMEM_BYTES),
    )(*operands, *[in_hbm(table) for table in tables])


def row_scratch(blocks, rows, terms, width, tables):
    return [
        pltpu.VMEM((4, blocks, rows, terms, LANES), jnp.float32),
        pltpu.VMEM((2 * blocks * rows * terms, 6 * LANES), jnp.bfloat16),
        pltpu.VMEM((2, width // LANES, LANES), jnp.float32),
        pltpu.VMEM((4, terms, width), jnp.float32),
        *[pltpu.VMEM(table.shape, table.dtype) for table in tables],
        pltpu.SemaphoreType.DMA((len(tables),)),
    ]


def spectra_by_exchange(density, blocks, groups, columns, row_factors, tables):
    rows_here, width = density.shape
    comps, ranks = lax.axis_size("comp"), lax.axis_size("rank")
    part = width // ranks
    lines = comps // 2
    terms = row_factors[0].shape[0]
    mine = lax.dynamic_slice_in_dim(density, lax.axis_index("rank") * part, part, 1)

    def along(block, step):
        pairs = [(c, ((c // 2 + step) % lines) * 2 + c % 2) for c in range(comps)]
        return lax.ppermute(block, "comp", pairs)

    def across(block):
        return lax.ppermute(block, "comp", [(c, c ^ 1) for c in range(comps)])

    def swapped(block, other):
        return lax.ppermute(block, "rank", [(r, r ^ other) for r in range(ranks)])

    def spectra(kernel, sources, operands, fetched):
        rows = rows_here * len(sources)
        (tile,) = whole_call(
            lambda *refs: kernel(blocks, groups, sources, *refs),
            [(2 * blocks, 2, rows, terms, LANES)],
            row_scratch(blocks, rows, terms, width, fetched),
            (*operands, *row_factors),
            fetched,
        )
        return tile

    def joined_spectra(pieces, sources):
        def kernel(blocks, groups, sources, *refs):
            pieces_kernel(blocks, groups, sources, len(pieces), *refs)

        return spectra(kernel, sources, (*pieces, *columns), tables)

    own_source = (None, 0, False)
    early = [(0, True)] + [(step, False) for step in range(1, lines)]
    late = [(step, True) for step in range(1, lines)]

    def quartered(places):
        return [(tuple((q, k) for q in range(4)), *place) for k, place in enumerate(places)]

    lined = [along(mine, step) for step in range(1, lines)]
    flipped_own = across(mine)
    own = spectra(own_kernel, [own_source], (), (*tables, density, *columns))
    (lined[lines // 2 - 1],) = after([lined[lines // 2 - 1]], own)
    near = jnp.stack([flipped_own, *lined])
    flipped = across(jnp.stack(lined))
    beyond = swapped(near, 2)
    ready = [near, beyond, swapped(near, 1), swapped(beyond, 1)]
    flipped_beyond = swapped(flipped, 2)
    flipped_beside = swapped(flipped, 1)
    first = joined_spectra(ready, quartered(early))
    (flipped_beyond,) = after([flipped_beyond], first)
    second = joined_spectra(
        [flipped, flipped_beyond, flipped_beside, swapped(flipped_beyond, 1)], quartered(late)
    )
    layout = [own_source[1:]] + early + late
    return [own[None], first[None], second[None]], layout


def spectra_by_gather(density, blocks, groups, columns, row_factors, tables):
    rows_here, width = density.shape
    comps, ranks = lax.axis_size("comp"), lax.axis_size("rank")
    terms = row_factors[0].shape[0]
    total_rows = rows_here * comps
    part = width // ranks
    mine = lax.dynamic_slice_in_dim(density, lax.axis_index("rank") * part, part, 1)
    gathered = lax.all_gather(mine, AXES, axis=0).reshape(comps, ranks, rows_here, part)
    tile_shape = (2 * blocks, 2, 8, terms, LANES)
    spectra = pl.pallas_call(
        lambda *refs: gathered_kernel(blocks, groups, *refs),
        grid=(total_rows // 8,),
        out_shape=jax.ShapeDtypeStruct((total_rows // 8, *tile_shape), jnp.float32),
        in_specs=[pl.BlockSpec((8 // rows_here, ranks, rows_here, part), lambda t: (t, 0, 0, 0))]
        + [pl.BlockSpec(memory_space=pltpu.VMEM)] * 4
        + [pl.BlockSpec(memory_space=pltpu.HBM)] * len(tables),
        out_specs=pl.BlockSpec((1, *tile_shape), lambda t: (t, 0, 0, 0, 0, 0)),
        scratch_shapes=row_scratch(blocks, 8, terms, width, tables),
        compiler_params=pltpu.CompilerParams(vmem_limit_bytes=VMEM_BYTES),
    )(gathered, *columns, *row_factors, *[in_hbm(table) for table in tables])
    return [spectra], None


def body(density, row_left, col_left, row_right, col_right):
    rows_here, width = density.shape
    comps = lax.axis_size("comp")
    devices = comps * lax.axis_size("rank")
    total_rows = rows_here * comps
    terms = row_left.shape[0]
    groups = min(devices, width // LANES)
    term_groups = devices // groups
    blocks = width // (groups * LANES)
    device_at = lax.axis_index(AXES)
    if term_groups > 1:
        term_at = lax.broadcasted_iota(jnp.int32, (terms, 1), 0)
        chosen = lax.div(term_at, terms // term_groups) == lax.div(device_at, groups)
        col_left = jnp.where(chosen, col_left, 0.0)
        col_right = jnp.where(chosen, col_right, 0.0)
    columns = (col_left, col_right)
    row_factors = (row_left, row_right)
    tables = (block_twiddles(blocks), split_rows(forward_table()))
    spectra = spectra_by_exchange if comps <= 8 else spectra_by_gather
    tiles, layout = spectra(density, blocks, groups, columns, row_factors, tables)

    out_rows = total_rows * 2 * blocks
    (sent,) = whole_call(
        lambda *refs: convolve_kernel(blocks, rows_here, layout, len(tiles), *refs),
        [(out_rows, LANES)],
        [
            pltpu.VMEM((2 * blocks, 3, PAD + total_rows, terms, LANES), jnp.float32),
            pltpu.VMEM((out_rows, terms, LANES), jnp.float32),
            pltpu.VMEM((out_rows, 2 * LANES), jnp.float32),
        ],
        (*tiles, split_rows(inverse_table())),
    )
    spread = lax.all_to_all(sent, AXES, split_axis=0, concat_axis=0, tiled=True)
    inner_cos, inner_sin, outer_table = final_tables(devices, groups, blocks, width)
    scaling = 0.5 / (math.sqrt(total_rows * width) * width)
    (result,) = whole_call(
        lambda *refs: final_kernel(scaling, *refs),
        [(width // LANES, LANES)],
        [],
        (
            spread,
            jnp.asarray(inner_cos, jnp.float32),
            jnp.asarray(inner_sin, jnp.float32),
            split_columns(outer_table),
        ),
        kept=False,
    )
    return result.reshape(1, width)


def solution(mesh):
    return jax.shard_map(
        body,
        mesh=mesh,
        in_specs=(P("comp", None), P(), P(), P(), P()),
        out_specs=P(AXES, None),
        check_vma=False,
    )
```

profile of v0, /device:TPU:0, one launch (start us, length us, event | category | flops | bytes accessed | tf_op | source)
XLA Modules:
  0.0 47.4 jit_solution(8289077184699592522)
XLA Ops:
  0.0 0.0 copy-start.6
  0.0 0.0 copy-start.7
  0.0 0.9 %constant_dynamic-slice_fusion = f32[4,4096]{1,0:T(4,128)S(1)} fusion(f32[4,16384]{1,0:T(4,128)} %refs_4_.3, s32[]{:T(128)S(6)} %select_n.3), kind=kLoop, calls=%fused_computation.2 | loop fusion | bytes 131076 | tf_op jit(solution)/shard_map/dynamic_slice | solution.py:476
  0.9 4.0 %collective-permute-start.2 = (f32[4,4096]{1,0:T(4,128)S(1)}, f32[4,4096]{1,0:T(4,128)S(1)}, u32[]{:S(2)}, u32[]{:S(2)}) collective-permute-start(f32[4,4096]{1,0:T(4,128)S(1)} %constant_dynamic-slice_fusion), channel_id=1, source_target_pairs={{0,16},{4,20},{8,24},{12,28},{16,0},{20,4},{24,8},{28,12},{1,17},{... | collective-permute-start | bytes 196616 | tf_op jit(solution)/shard_map/ppermute | solution.py:480
  4.9 1.6 %collective-permute-start.1 = (f32[4,4096]{1,0:T(4,128)S(1)}, f32[4,4096]{1,0:T(4,128)S(1)}, u32[]{:S(2)}, u32[]{:S(2)}) collective-permute-start(f32[4,4096]{1,0:T(4,128)S(1)} %constant_dynamic-slice_fusion), channel_id=1, source_target_pairs={{0,8},{4,12},{8,16},{12,20},{16,24},{20,28},{24,0},{28,4},{1,9},{5... | collective-permute-start | bytes 196616 | tf_op jit(solution)/shard_map/ppermute | solution.py:480
  6.5 2.2 %collective-permute-start.3 = (f32[4,4096]{1,0:T(4,128)S(1)}, f32[4,4096]{1,0:T(4,128)S(1)}, u32[]{:S(2)}, u32[]{:S(2)}) collective-permute-start(f32[4,4096]{1,0:T(4,128)S(1)} %constant_dynamic-slice_fusion), channel_id=1, source_target_pairs={{0,24},{4,28},{8,0},{12,4},{16,8},{20,12},{24,16},{28,20},{1,25},{... | collective-permute-start | bytes 196616 | tf_op jit(solution)/shard_map/ppermute | solution.py:480
  8.7 1.5 %collective-permute-start = (f32[4,4096]{1,0:T(4,128)S(1)}, f32[4,4096]{1,0:T(4,128)S(1)}, u32[]{:S(2)}, u32[]{:S(2)}) collective-permute-start(f32[4,4096]{1,0:T(4,128)S(1)} %constant_dynamic-slice_fusion), channel_id=1, source_target_pairs={{0,4},{4,0},{8,12},{12,8},{16,20},{20,16},{24,28},{28,24},{1,5},{5... | collective-permute-start | bytes 196616 | tf_op jit(solution)/shard_map/ppermute | solution.py:483
  10.3 0.0 copy-done.6
  10.3 0.0 copy-done.7
  10.3 3.1 %shard_map.109.refs_1_ = f32[8,2,4,8,128]{4,3,2,1,0:T(8,128)S(1)} custom-call(f32[8,32]{1,0:T(8,128)S(1)} %copy-done.6, f32[8,32]{1,0:T(8,128)S(1)} %copy-done.7, f32[4,2,8,128]{3,2,1,0:T(8,128)} %constant.22.clone.refs_2_.refs_8_, bf16[768,256]{1,0:T(8,128)(2,1)} %constant.33.refs_3_.refs_9_, f32[4,16384]{1,0:T(4,128)} %refs_4_.3, f32[8,16384]{1,0:T(8,128)} %refs_4_.5, ...), custom_call_target="tpu_custom_call" | custom-call | tf_op jit(solution)/shard_map/pallas_call | solution.py:448
  13.3 0.0 collective-permute-done.2.refs_0_
  13.3 0.0 copy-start.1
  13.4 0.0 copy-start
  13.4 0.0 collective-permute-done.1
  13.4 0.0 collective-permute-done.3
  13.4 0.0 collective-permute-done
  13.4 0.1 pad_maximum_fusion.refs_0_
  13.5 1.6 %collective-permute-start.4 = (f32[4,4,4096]{2,1,0:T(4,128)S(1)}, f32[4,4,4096]{2,1,0:T(4,128)S(1)}, u32[]{:S(2)}, u32[]{:S(2)}) collective-permute-start(f32[4,4,4096]{2,1,0:T(4,128)S(1)} %pad_maximum_fusion.refs_0_), channel_id=1, source_target_pairs={{0,2},{1,3},{2,0},{3,1},{4,6},{5,7},{6,4},{7,5},{8,10},{9,11},{10,... | collective-permute-start | bytes 786440 | tf_op jit(solution)/shard_map/ppermute | solution.py:486
  15.1 1.2 %collective-permute-start.7 = (f32[3,4,4096]{2,1,0:T(4,128)S(1)}, f32[3,4,4096]{2,1,0:T(4,128)S(1)}, u32[]{:S(2)}, u32[]{:S(2)}) collective-permute-start(f32[3,4,4096]{2,1,0:T(4,128)S(1)} %pad_maximum_fusion.1), channel_id=1, source_target_pairs={{0,4},{4,0},{8,12},{12,8},{16,20},{20,16},{24,28},{28,24},{1,5},{5... | collective-permute-start | bytes 589832 | tf_op jit(solution)/shard_map/ppermute | solution.py:483
  16.3 0.0 collective-permute-start.5
  16.3 4.2 %collective-permute-done.4.refs_1_ = f32[4,4,4096]{2,1,0:T(4,128)S(1)} collective-permute-done((f32[4,4,4096]{2,1,0:T(4,128)S(1)}, f32[4,4,4096]{2,1,0:T(4,128)S(1)}, u32[]{:S(2)}, u32[]{:S(2)}) %collective-permute-start.4) | collective-permute-done | bytes 262176 | tf_op jit(solution)/shard_map/ppermute | solution.py:486
  20.5 0.0 collective-permute-start.6
  20.5 0.3 collective-permute-done.7.refs_0_
  20.8 1.2 %collective-permute-start.8 = (f32[3,4,4096]{2,1,0:T(4,128)S(1)}, f32[3,4,4096]{2,1,0:T(4,128)S(1)}, u32[]{:S(2)}, u32[]{:S(2)}) collective-permute-start(f32[3,4,4096]{2,1,0:T(4,128)S(1)} %collective-permute-done.7.refs_0_), channel_id=1, source_target_pairs={{0,2},{1,3},{2,0},{3,1},{4,6},{5,7},{6,4},{7,5},{8,10},{9,11},{10,... | collective-permute-start | bytes 589832 | tf_op jit(solution)/shard_map/ppermute | solution.py:486
  22.0 0.2 collective-permute-start.9
  22.2 0.0 collective-permute-done.5.refs_2_
  22.2 0.0 collective-permute-done.6.refs_3_
  22.2 0.0 copy-done.1
  22.2 0.0 copy-done
  22.2 3.8 %shard_map.111.refs_1_ = f32[8,2,16,8,128]{4,3,2,1,0:T(8,128)S(1)} custom-call(f32[4,4,4096]{2,1,0:T(4,128)S(1)} %pad_maximum_fusion.refs_0_, f32[4,4,4096]{2,1,0:T(4,128)S(1)} %collective-permute-done.4.refs_1_, f32[4,4,4096]{2,1,0:T(4,128)S(1)} %collective-permute-done.5.refs_2_, f32[4,4,4096]{2,1,0:T(4,128)S(1)} %collective-permute-done.6.refs_3_, ...), custom_call_target="tpu_custom_call" | custom-call | tf_op jit(solution)/shard_map/pallas_call | solution.py:448
  26.0 1.8 %collective-permute-done.8.refs_0_ = f32[3,4,4096]{2,1,0:T(4,128)S(1)} collective-permute-done((f32[3,4,4096]{2,1,0:T(4,128)S(1)}, f32[3,4,4096]{2,1,0:T(4,128)S(1)}, u32[]{:S(2)}, u32[]{:S(2)}) %collective-permute-start.8) | collective-permute-done | bytes 196640 | tf_op jit(solution)/shard_map/ppermute | solution.py:486
  27.8 0.0 copy-start.3
  27.8 0.0 collective-permute-start.10
  27.8 0.0 collective-permute-done.9.refs_2_
  27.8 1.4 %collective-permute-done.10.refs_3_ = f32[3,4,4096]{2,1,0:T(4,128)S(1)} collective-permute-done((f32[3,4,4096]{2,1,0:T(4,128)S(1)}, f32[3,4,4096]{2,1,0:T(4,128)S(1)}, u32[]{:S(2)}, u32[]{:S(2)}) %collective-permute-start.10) | collective-permute-done | bytes 196640 | tf_op jit(solution)/shard_map/ppermute | solution.py:486
  29.2 3.0 %shard_map.113 = f32[8,2,12,8,128]{4,3,2,1,0:T(8,128)S(1)} custom-call(f32[3,4,4096]{2,1,0:T(4,128)S(1)} %collective-permute-done.7.refs_0_, f32[3,4,4096]{2,1,0:T(4,128)S(1)} %shard_map.112.refs_1_, f32[3,4,4096]{2,1,0:T(4,128)S(1)} %collective-permute-done.9.refs_2_, f32[3,4,4096]{2,1,0:T(4,128)S(1)} %collective-permute-done.10.refs_3_, ...), custom_call_target="tpu_custom_call" | custom-call | tf_op jit(solution)/shard_map/pallas_call | solution.py:448
  32.3 0.0 copy-done.3
  32.3 0.0 copy-start.2
  32.3 2.9 %shard_map.114 = f32[256,128]{1,0:T(8,128)S(1)} custom-call(f32[1,8,2,4,8,128]{5,4,3,2,1,0:T(8,128)S(1)} %bitcast.12, f32[1,8,2,16,8,128]{5,4,3,2,1,0:T(8,128)S(1)} %bitcast.10, f32[1,8,2,12,8,128]{5,4,3,2,1,0:T(8,128)S(1)} %bitcast.11, bf16[768,128]{1,0:T(8,128)(2,1)S(1)} %copy-done.3), custom_call_target="tpu_custom_call" | custom-call | tf_op jit(solution)/shard_map/pallas_call | solution.py:448
  35.2 0.0 copy-start.4
  35.2 0.0 copy-start.5
  35.2 11.3 %all_to_all.11 = f32[32,8,128]{2,1,0:T(8,128)S(1)} all-to-all(f32[32,8,128]{2,1,0:T(8,128)S(1)} %bitcast.15), channel_id=1, replica_groups=mesh['comp'=8,'rank'=4] {'comp','rank'}, dimensions={0} | all-to-all | bytes 262144 | tf_op jit(solution)/shard_map/all_to_all | solution.py:586
  46.5 0.0 copy-done.2
  46.5 0.0 copy-done.4
  46.5 0.0 copy-done.5
  46.5 0.9 %shard_map.115 = f32[128,128]{1,0:T(8,128)} custom-call(f32[256,128]{1,0:T(8,128)S(1)} %bitcast.16, f32[256,128]{1,0:T(8,128)S(1)} %copy-done.4, f32[256,128]{1,0:T(8,128)S(1)} %copy-done.5, bf16[128,1536]{1,0:T(8,128)(2,1)S(1)} %copy-done.2), custom_call_target="tpu_custom_call" | custom-call | tf_op jit(solution)/shard_map/pallas_call | solution.py:448
  (3 shorter events, 0.0 us)
Async XLA Ops:
  0.0 10.3 %copy-start.6 = (f32[8,32]{1,0:T(8,128)S(1)}, f32[8,32]{1,0:T(8,128)}, u32[]{:S(2)}) copy-start(f32[8,32]{1,0:T(8,128)} %refs_6_.5) | copy-start | bytes 3076
  0.0 10.3 %copy-start.7 = (f32[8,32]{1,0:T(8,128)S(1)}, f32[8,32]{1,0:T(8,128)}, u32[]{:S(2)}) copy-start(f32[8,32]{1,0:T(8,128)} %refs_7_.3) | copy-start | bytes 3076
  0.9 12.5 %collective-permute-start.2 = (f32[4,4096]{1,0:T(4,128)S(1)}, f32[4,4096]{1,0:T(4,128)S(1)}, u32[]{:S(2)}, u32[]{:S(2)}) collective-permute-start(f32[4,4096]{1,0:T(4,128)S(1)} %constant_dynamic-slice_fusion), channel_id=1, source_target_pairs={{0,16},{4,20},{8,24},{12,28},{16,0},{20,4},{24,8},{28,12},{1,17},{... | collective-permute-start | bytes 196616 | tf_op jit(solution)/shard_map/ppermute | solution.py:480
  4.9 8.5 %collective-permute-start.1 = (f32[4,4096]{1,0:T(4,128)S(1)}, f32[4,4096]{1,0:T(4,128)S(1)}, u32[]{:S(2)}, u32[]{:S(2)}) collective-permute-start(f32[4,4096]{1,0:T(4,128)S(1)} %constant_dynamic-slice_fusion), channel_id=1, source_target_pairs={{0,8},{4,12},{8,16},{12,20},{16,24},{20,28},{24,0},{28,4},{1,9},{5... | collective-permute-start | bytes 196616 | tf_op jit(solution)/shard_map/ppermute | solution.py:480
  6.5 6.9 %collective-permute-start.3 = (f32[4,4096]{1,0:T(4,128)S(1)}, f32[4,4096]{1,0:T(4,128)S(1)}, u32[]{:S(2)}, u32[]{:S(2)}) collective-permute-start(f32[4,4096]{1,0:T(4,128)S(1)} %constant_dynamic-slice_fusion), channel_id=1, source_target_pairs={{0,24},{4,28},{8,0},{12,4},{16,8},{20,12},{24,16},{28,20},{1,25},{... | collective-permute-start | bytes 196616 | tf_op jit(solution)/shard_map/ppermute | solution.py:480
  8.7 4.7 %collective-permute-start = (f32[4,4096]{1,0:T(4,128)S(1)}, f32[4,4096]{1,0:T(4,128)S(1)}, u32[]{:S(2)}, u32[]{:S(2)}) collective-permute-start(f32[4,4096]{1,0:T(4,128)S(1)} %constant_dynamic-slice_fusion), channel_id=1, source_target_pairs={{0,4},{4,0},{8,12},{12,8},{16,20},{20,16},{24,28},{28,24},{1,5},{5... | collective-permute-start | bytes 196616 | tf_op jit(solution)/shard_map/ppermute | solution.py:483
  13.3 8.9 %copy-start.1 = (f32[8,16384]{1,0:T(8,128)S(1)}, f32[8,16384]{1,0:T(8,128)}, u32[]{:S(2)}) copy-start(f32[8,16384]{1,0:T(8,128)} %refs_5_.5) | copy-start | bytes 1572868
  13.4 8.8 %copy-start = (f32[8,16384]{1,0:T(8,128)S(1)}, f32[8,16384]{1,0:T(8,128)}, u32[]{:S(2)}) copy-start(f32[8,16384]{1,0:T(8,128)} %refs_4_.5) | copy-start | bytes 1572868
  13.5 7.0 %collective-permute-start.4 = (f32[4,4,4096]{2,1,0:T(4,128)S(1)}, f32[4,4,4096]{2,1,0:T(4,128)S(1)}, u32[]{:S(2)}, u32[]{:S(2)}) collective-permute-start(f32[4,4,4096]{2,1,0:T(4,128)S(1)} %pad_maximum_fusion.refs_0_), channel_id=1, source_target_pairs={{0,2},{1,3},{2,0},{3,1},{4,6},{5,7},{6,4},{7,5},{8,10},{9,11},{10,... | collective-permute-start | bytes 786440 | tf_op jit(solution)/shard_map/ppermute | solution.py:486
  15.1 5.7 %collective-permute-start.7 = (f32[3,4,4096]{2,1,0:T(4,128)S(1)}, f32[3,4,4096]{2,1,0:T(4,128)S(1)}, u32[]{:S(2)}, u32[]{:S(2)}) collective-permute-start(f32[3,4,4096]{2,1,0:T(4,128)S(1)} %pad_maximum_fusion.1), channel_id=1, source_target_pairs={{0,4},{4,0},{8,12},{12,8},{16,20},{20,16},{24,28},{28,24},{1,5},{5... | collective-permute-start | bytes 589832 | tf_op jit(solution)/shard_map/ppermute | solution.py:483
  16.3 5.9 %collective-permute-start.5 = (f32[4,4,4096]{2,1,0:T(4,128)S(1)}, f32[4,4,4096]{2,1,0:T(4,128)S(1)}, u32[]{:S(2)}, u32[]{:S(2)}) collective-permute-start(f32[4,4,4096]{2,1,0:T(4,128)S(1)} %pad_maximum_fusion.refs_0_), channel_id=1, source_target_pairs={{0,1},{1,0},{2,3},{3,2},{4,5},{5,4},{6,7},{7,6},{8,9},{9,8},{10,11... | collective-permute-start | bytes 786440 | tf_op jit(solution)/shard_map/ppermute | solution.py:486
  20.5 1.7 %collective-permute-start.6 = (f32[4,4,4096]{2,1,0:T(4,128)S(1)}, f32[4,4,4096]{2,1,0:T(4,128)S(1)}, u32[]{:S(2)}, u32[]{:S(2)}) collective-permute-start(f32[4,4,4096]{2,1,0:T(4,128)S(1)} %collective-permute-done.4.refs_1_), channel_id=1, source_target_pairs={{0,1},{1,0},{2,3},{3,2},{4,5},{5,4},{6,7},{7,6},{8,9},{9,8},{10,11... | collective-permute-start | bytes 786440 | tf_op jit(solution)/shard_map/ppermute | solution.py:486
  20.8 7.0 %collective-permute-start.8 = (f32[3,4,4096]{2,1,0:T(4,128)S(1)}, f32[3,4,4096]{2,1,0:T(4,128)S(1)}, u32[]{:S(2)}, u32[]{:S(2)}) collective-permute-start(f32[3,4,4096]{2,1,0:T(4,128)S(1)} %collective-permute-done.7.refs_0_), channel_id=1, source_target_pairs={{0,2},{1,3},{2,0},{3,1},{4,6},{5,7},{6,4},{7,5},{8,10},{9,11},{10,... | collective-permute-start | bytes 589832 | tf_op jit(solution)/shard_map/ppermute | solution.py:486
  22.0 5.8 %collective-permute-start.9 = (f32[3,4,4096]{2,1,0:T(4,128)S(1)}, f32[3,4,4096]{2,1,0:T(4,128)S(1)}, u32[]{:S(2)}, u32[]{:S(2)}) collective-permute-start(f32[3,4,4096]{2,1,0:T(4,128)S(1)} %collective-permute-done.7.refs_0_), channel_id=1, source_target_pairs={{0,1},{1,0},{2,3},{3,2},{4,5},{5,4},{6,7},{7,6},{8,9},{9,8},{10,11... | collective-permute-start | bytes 589832 | tf_op jit(solution)/shard_map/ppermute | solution.py:486
  27.8 4.5 %copy-start.3 = (bf16[768,128]{1,0:T(8,128)(2,1)S(1)}, bf16[768,128]{1,0:T(8,128)(2,1)}, u32[]{:S(2)}) copy-start(bf16[768,128]{1,0:T(8,128)(2,1)} %constant.38.refs_3_) | copy-start | bytes 589828
  27.8 1.4 %collective-permute-start.10 = (f32[3,4,4096]{2,1,0:T(4,128)S(1)}, f32[3,4,4096]{2,1,0:T(4,128)S(1)}, u32[]{:S(2)}, u32[]{:S(2)}) collective-permute-start(f32[3,4,4096]{2,1,0:T(4,128)S(1)} %shard_map.112.refs_1_), channel_id=1, source_target_pairs={{0,1},{1,0},{2,3},{3,2},{4,5},{5,4},{6,7},{7,6},{8,9},{9,8},{10,11... | collective-permute-start | bytes 589832 | tf_op jit(solution)/shard_map/ppermute | solution.py:486
  32.3 14.2 %copy-start.2 = (bf16[128,1536]{1,0:T(8,128)(2,1)S(1)}, bf16[128,1536]{1,0:T(8,128)(2,1)}, u32[]{:S(2)}) copy-start(bf16[128,1536]{1,0:T(8,128)(2,1)} %constant.43.refs_3_) | copy-start | bytes 1179652
  35.2 11.3 %copy-start.4 = (f32[256,128]{1,0:T(8,128)S(1)}, f32[256,128]{1,0:T(8,128)}, u32[]{:S(2)}) copy-start(f32[256,128]{1,0:T(8,128)} %constant.25.clone.refs_1_) | copy-start | bytes 393220
  35.2 11.3 %copy-start.5 = (f32[256,128]{1,0:T(8,128)S(1)}, f32[256,128]{1,0:T(8,128)}, u32[]{:S(2)}) copy-start(f32[256,128]{1,0:T(8,128)} %constant.26.clone.refs_2_) | copy-start | bytes 393220
where the time goes:
time: 47.6 us; the launch traced here: 47.4 us
  Pallas kernels  13.6 us (29%)
  starting transfers between devices  13.5 us (28%)
  blocking collectives  11.3 us (24%)
  waiting for transfers between devices  7.78 us (16%)
  local copies, waits for them, and re-layouts  0.92 us (2%)
    pallas_call x5, Pallas kernels, whole_call(): pl.pallas_call(kernel, out_shape=[out_type(shape, jnp.float32) for shape...  13.6 us
    all_to_all x1, blocking collectives, body(): spread = lax.all_to_all(sent, AXES, split_axis=0, concat_axis=0, tiled=True)  11.3 us
    ppermute x3, starting transfers between devices, along(): return lax.ppermute(block, 'comp', pairs)  7.86 us
    ppermute x6, waiting for transfers between devices, swapped(): return lax.ppermute(block, 'rank', [(r, r ^ other) for r in range(ranks)])  7.43 us
    ppermute x6, starting transfers between devices, swapped(): return lax.ppermute(block, 'rank', [(r, r ^ other) for r in range(ranks)])  2.94 us
    ppermute x2, starting transfers between devices, across(): return lax.ppermute(block, 'comp', [(c, c ^ 1) for c in range(comps)])  2.7 us
  transfers between devices with their start and end apart: 11, of which 4 were waited for; matrix products, arithmetic and copies ran while one was open for 0% of the time, Pallas kernels for 14%

commit v1 on v0

--- a/solution.py
+++ b/solution.py
@@ -93,13 +93,17 @@
     )
 
 
-def reduce_rows(blocks, rows, terms, fetch, factors_at, starts, span, partial):
+def reduce_rows(blocks, rows, terms, fetch, factors_at, starts, span, partial, before=None):
     inner = blocks * LANES
     outer = span // inner
     unroll = math.gcd(16, outer)
 
     def reduce_block(block, first, count):
         sums = (jnp.zeros((terms, LANES), jnp.float32),) * (4 * count)
+        if before is not None:
+            sums = tuple(
+                before[k, block, first + row] for row in range(count) for k in range(4)
+            )
         for part, start in enumerate(starts):
 
             def step(at, sums, part=part, start=start):
@@ -242,7 +246,7 @@
 
 
 def own_kernel(blocks, groups, sources, *refs):
-    row_factors, sent, refs = refs[0:2], refs[2:7], refs[7:]
+    row_factors, sent, refs = refs[1:3], refs[3:8], refs[8:]
     out, partial, joined, phases, weights = refs[:5]
     held, arrivals = refs[5:10], refs[10]
     copies = start_tables(sent, held, arrivals)
@@ -256,25 +260,71 @@
     )
 
 
-def reduce_pieces(blocks, sources, pieces, columns, phases, weights, partial):
+def reduce_pieces(
+    blocks, sources, pieces, columns, phases, weights, partial, parts=(0, 1, 2, 3)
+):
     rows_here = pieces[0].shape[-2]
     terms, width = columns[0].shape
     ranks = lax.axis_size("rank")
     span = width // ranks
     rank_at = lax.axis_index("rank")
-    starts = [(rank_at ^ other) * span for other in HELD_PARTS]
+    starts = [(rank_at ^ HELD_PARTS[part]) * span for part in parts]
 
     def fetch(part, row, lane):
         quarters, _, _ = sources[row // rows_here]
         row = pl.ds(row % rows_here, 1)
         if quarters is None:
             return pieces[0][row, pl.ds(pl.multiple_of(starts[part] + lane, LANES), LANES)]
-        number, index = quarters[part]
+        number, index = quarters[parts[part]]
         return pieces[number][index, row, pl.ds(pl.multiple_of(lane, LANES), LANES)]
 
     factors_at = made_factors(columns, phases, weights)
     rows = len(sources) * rows_here
     reduce_rows(blocks, rows, terms, fetch, factors_at, starts, span, partial)
+
+
+def ahead_kernel(blocks, groups, sources, *refs):
+    pieces, columns, (partial, quarter, phases, weights) = refs[0:3], refs[3:5], refs[5:]
+    make_phases(groups, phases)
+    reduce_pieces(
+        blocks, sources, pieces, columns, phases, weights, partial, parts=(0, 1, 2)
+    )
+    factors_at = made_factors(columns, phases, weights)
+    span = quarter.shape[2]
+    start = (lax.axis_index("rank") ^ HELD_PARTS[3]) * span
+
+    def weigh(at, carry):
+        lane = at * LANES
+        for k, factor in enumerate(factors_at(start + lane, True)):
+            quarter[k, :, pl.ds(pl.multiple_of(lane, LANES), LANES)] = factor
+        return carry
+
+    lax.fori_loop(0, span // LANES, weigh, 0, unroll=4)
+
+
+def last_kernel(blocks, groups, sources, *refs):
+    del groups
+    piece, before, quarter = refs[0:3]
+    row_factors, tables, refs = refs[3:5], refs[5:7], refs[7:]
+    out, partial, joined, _, _, twiddle, table, arrivals = refs
+    copies = start_tables(tables, (twiddle, table), arrivals)
+    rows_here = piece.shape[-2]
+    terms, span = quarter.shape[1:]
+
+    def fetch(part, row, lane):
+        _, index = sources[row // rows_here][0][3]
+        place = pl.ds(pl.multiple_of(lane, LANES), LANES)
+        return piece[index, pl.ds(row % rows_here, 1), place]
+
+    def factors_at(lane, first):
+        place = pl.ds(pl.multiple_of(lane, LANES), LANES)
+        return [quarter[k, :, place] for k in range(4)]
+
+    rows = len(sources) * rows_here
+    reduce_rows(blocks, rows, terms, fetch, factors_at, [0], span, partial, before)
+    finish_pieces(
+        blocks, sources, copies, row_factors, twiddle, table, out, partial, joined
+    )
 
 
 def finish_pieces(blocks, sources, copies, row_factors, twiddle, table, out, partial, joined):
@@ -463,7 +513,7 @@
         pltpu.VMEM((2, width // LANES, LANES), jnp.float32),
         pltpu.VMEM((4, terms, width), jnp.float32),
         *[pltpu.VMEM(table.shape, table.dtype) for table in tables],
-        pltpu.SemaphoreType.DMA((len(tables),)),
+        *([pltpu.SemaphoreType.DMA((len(tables),))] if tables else []),
     ]
 
 
@@ -510,20 +560,23 @@
         return [(tuple((q, k) for q in range(4)), *place) for k, place in enumerate(places)]
 
     lined = [along(mine, step) for step in range(1, lines)]
-    flipped_own = across(mine)
-    own = spectra(own_kernel, [own_source], (), (*tables, density, *columns))
-    (lined[lines // 2 - 1],) = after([lined[lines // 2 - 1]], own)
-    near = jnp.stack([flipped_own, *lined])
+    near = jnp.stack([across(mine), *lined])
     flipped = across(jnp.stack(lined))
-    beyond = swapped(near, 2)
-    ready = [near, beyond, swapped(near, 1), swapped(beyond, 1)]
-    flipped_beyond = swapped(flipped, 2)
-    flipped_beside = swapped(flipped, 1)
-    first = joined_spectra(ready, quartered(early))
+    beyond, beside = swapped(near, 2), swapped(near, 1)
+    flipped_beyond, flipped_beside = swapped(flipped, 2), swapped(flipped, 1)
+    own = spectra(own_kernel, [own_source], (near,), (*tables, density, *columns))
+    (beyond,) = after([beyond], own)
+    first = joined_spectra([near, beyond, beside, swapped(beyond, 1)], quartered(early))
     (flipped_beyond,) = after([flipped_beyond], first)
-    second = joined_spectra(
-        [flipped, flipped_beyond, flipped_beside, swapped(flipped_beyond, 1)], quartered(late)
-    )
+    late_sources = quartered(late)
+    ahead = whole_call(
+        lambda *refs: ahead_kernel(blocks, groups, late_sources, *refs),
+        [(4, blocks, rows_here * len(late), terms, LANES), (4, terms, part)],
+        row_scratch(blocks, rows_here, terms, width, ())[2:4],
+        (flipped, flipped_beyond, flipped_beside, *columns),
+    )
+    last = swapped(flipped_beyond, 1)
+    second = spectra(last_kernel, late_sources, (last, *ahead), tables)
     layout = [own_source[1:]] + early + late
     return [own[None], first[None], second[None]], layout
 

time: 47.6 us -> 48.6 us (1.021)
  Pallas kernels: 13.6 us -> 15.4 us
  starting transfers between devices: 13.5 us -> 12.4 us
  blocking collectives: 11.3 us -> 11.8 us
    ppermute x3, waiting for transfers between devices: 0.01 us -> 3.94 us  [along(): return lax.ppermute(block, 'comp', pairs)]
    ppermute x6, waiting for transfers between devices: 7.43 us -> 3.54 us  [swapped(): return lax.ppermute(block, 'rank', [(r, r ^ other) for r in range(ranks)])]
    ppermute x3, starting transfers between devices: 7.86 us -> 6.06 us  [along(): return lax.ppermute(block, 'comp', pairs)]
    pallas_call x5 -> x6, Pallas kernels: 13.6 us -> 15.4 us  [whole_call(): pl.pallas_call(kernel, out_shape=[out_type(shape, jnp.float32) for shape...]
    all_to_all x1, blocking collectives: 11.3 us -> 11.8 us  [body(): spread = lax.all_to_all(sent, AXES, split_axis=0, concat_axis=0, tiled=True)]
  transfers between devices with their start and end apart: 11 -> 11, of which waited for: 4 -> 3; matrix products, arithmetic and copies ran while one was open for 0% -> 0% of each run, Pallas kernels for 14% -> 20%
where the time goes in v1:
time: 48.6 us; the launch traced here: 48.4 us
  Pallas kernels  15.4 us (32%)
  starting transfers between devices  12.4 us (26%)
  blocking collectives  11.8 us (24%)
  waiting for transfers between devices  7.49 us (15%)
  local copies, waits for them, and re-layouts  0.9 us (2%)
    pallas_call x6, Pallas kernels, whole_call(): pl.pallas_call(kernel, out_shape=[out_type(shape, jnp.float32) for shape...  15.4 us
    all_to_all x1, blocking collectives, body(): spread = lax.all_to_all(sent, AXES, split_axis=0, concat_axis=0, tiled=True)  11.8 us
    ppermute x3, starting transfers between devices, along(): return lax.ppermute(block, 'comp', pairs)  6.06 us
    ppermute x3, waiting for transfers between devices, along(): return lax.ppermute(block, 'comp', pairs)  3.94 us
    ppermute x6, waiting for transfers between devices, swapped(): return lax.ppermute(block, 'rank', [(r, r ^ other) for r in range(ranks)])  3.54 us
    ppermute x6, starting transfers between devices, swapped(): return lax.ppermute(block, 'rank', [(r, r ^ other) for r in range(ranks)])  3.28 us
    ppermute x2, starting transfers between devices, across(): return lax.ppermute(block, 'comp', [(c, c ^ 1) for c in range(comps)])  3.1 us
  transfers between devices with their start and end apart: 11, of which 3 were waited for; matrix products, arithmetic and copies ran while one was open for 0% of the time, Pallas kernels for 20%

profile of v1, /device:TPU:0, one launch (start us, length us, event | category | flops | bytes accessed | tf_op | source)
XLA Modules:
  0.0 48.4 jit_solution(12896306855886554968)
XLA Ops:
  0.0 0.8 %constant_dynamic-slice_fusion = f32[4,4096]{1,0:T(4,128)S(1)} fusion(f32[4,16384]{1,0:T(4,128)} %refs_5_.3, s32[]{:T(128)S(6)} %select_n.3), kind=kLoop, calls=%fused_computation.2 | loop fusion | bytes 131076 | tf_op jit(solution)/shard_map/dynamic_slice | solution.py:526
  0.8 5.0 %collective-permute-start.3 = (f32[4,4096]{1,0:T(4,128)S(1)}, f32[4,4096]{1,0:T(4,128)S(1)}, u32[]{:S(2)}, u32[]{:S(2)}) collective-permute-start(f32[4,4096]{1,0:T(4,128)S(1)} %constant_dynamic-slice_fusion), channel_id=1, source_target_pairs={{0,24},{4,28},{8,0},{12,4},{16,8},{20,12},{24,16},{28,20},{1,25},{... | collective-permute-start | bytes 196616 | tf_op jit(solution)/shard_map/ppermute | solution.py:530
  5.9 0.0 collective-permute-start.2
  5.9 1.0 %collective-permute-start.1 = (f32[4,4096]{1,0:T(4,128)S(1)}, f32[4,4096]{1,0:T(4,128)S(1)}, u32[]{:S(2)}, u32[]{:S(2)}) collective-permute-start(f32[4,4096]{1,0:T(4,128)S(1)} %constant_dynamic-slice_fusion), channel_id=1, source_target_pairs={{0,8},{4,12},{8,16},{12,20},{16,24},{20,28},{24,0},{28,4},{1,9},{5... | collective-permute-start | bytes 196616 | tf_op jit(solution)/shard_map/ppermute | solution.py:530
  6.9 1.5 %collective-permute-start = (f32[4,4096]{1,0:T(4,128)S(1)}, f32[4,4096]{1,0:T(4,128)S(1)}, u32[]{:S(2)}, u32[]{:S(2)}) collective-permute-start(f32[4,4096]{1,0:T(4,128)S(1)} %constant_dynamic-slice_fusion), channel_id=1, source_target_pairs={{0,4},{4,0},{8,12},{12,8},{16,20},{20,16},{24,28},{28,24},{1,5},{5... | collective-permute-start | bytes 196616 | tf_op jit(solution)/shard_map/ppermute | solution.py:533
  8.4 0.0 collective-permute-done.3
  8.4 3.9 %collective-permute-done.2 = f32[4,4096]{1,0:T(4,128)S(1)} collective-permute-done((f32[4,4096]{1,0:T(4,128)S(1)}, f32[4,4096]{1,0:T(4,128)S(1)}, u32[]{:S(2)}, u32[]{:S(2)}) %collective-permute-start.2) | collective-permute-done | bytes 65568 | tf_op jit(solution)/shard_map/ppermute | solution.py:530
  12.4 0.0 collective-permute-done.1
  12.4 0.0 collective-permute-done
  12.4 0.1 pad_maximum_fusion.refs_0_
  12.4 0.0 copy-start.6
  12.4 0.0 copy-start.7
  12.5 1.6 %collective-permute-start.4 = (f32[4,4,4096]{2,1,0:T(4,128)S(1)}, f32[4,4,4096]{2,1,0:T(4,128)S(1)}, u32[]{:S(2)}, u32[]{:S(2)}) collective-permute-start(f32[4,4,4096]{2,1,0:T(4,128)S(1)} %pad_maximum_fusion.refs_0_), channel_id=1, source_target_pairs={{0,2},{1,3},{2,0},{3,1},{4,6},{5,7},{6,4},{7,5},{8,10},{9,11},{10,... | collective-permute-start | bytes 786440 | tf_op jit(solution)/shard_map/ppermute | solution.py:536
  14.1 1.6 %collective-permute-start.7 = (f32[3,4,4096]{2,1,0:T(4,128)S(1)}, f32[3,4,4096]{2,1,0:T(4,128)S(1)}, u32[]{:S(2)}, u32[]{:S(2)}) collective-permute-start(f32[3,4,4096]{2,1,0:T(4,128)S(1)} %pad_maximum_fusion.1), channel_id=1, source_target_pairs={{0,4},{4,0},{8,12},{12,8},{16,20},{20,16},{24,28},{28,24},{1,5},{5... | collective-permute-start | bytes 589832 | tf_op jit(solution)/shard_map/ppermute | solution.py:533
  15.7 0.0 collective-permute-start.5
  15.7 0.0 copy-done.6
  15.7 0.0 copy-done.7
  15.7 0.0 copy-start.1
  15.7 3.1 %shard_map.109.refs_1_ = f32[8,2,4,8,128]{4,3,2,1,0:T(8,128)S(1)} custom-call(f32[4,4,4096]{2,1,0:T(4,128)S(1)} %pad_maximum_fusion.refs_0_, f32[8,32]{1,0:T(8,128)S(1)} %copy-done.6, f32[8,32]{1,0:T(8,128)S(1)} %copy-done.7, f32[4,2,8,128]{3,2,1,0:T(8,128)} %constant.22.clone.refs_3_.refs_8_.refs_5_, bf16[768,256]{1,0:T(8,128)(2,1)} %constant.33.refs_4_.refs_9_.refs_6_, ...), custom_call_target="tpu_custom_call" | custom-call | tf_op jit(solution)/shard_map/pallas_call | solution.py:498
  18.8 0.0 copy-start
  18.8 1.8 %collective-permute-done.4.refs_0_ = f32[4,4,4096]{2,1,0:T(4,128)S(1)} collective-permute-done((f32[4,4,4096]{2,1,0:T(4,128)S(1)}, f32[4,4,4096]{2,1,0:T(4,128)S(1)}, u32[]{:S(2)}, u32[]{:S(2)}) %collective-permute-start.4) | collective-permute-done | bytes 262176 | tf_op jit(solution)/shard_map/ppermute | solution.py:536
  20.6 0.0 collective-permute-start.6
  20.6 0.0 collective-permute-done.7.refs_0_
  20.6 1.6 %collective-permute-start.8 = (f32[3,4,4096]{2,1,0:T(4,128)S(1)}, f32[3,4,4096]{2,1,0:T(4,128)S(1)}, u32[]{:S(2)}, u32[]{:S(2)}) collective-permute-start(f32[3,4,4096]{2,1,0:T(4,128)S(1)} %collective-permute-done.7.refs_0_), channel_id=1, source_target_pairs={{0,2},{1,3},{2,0},{3,1},{4,6},{5,7},{6,4},{7,5},{8,10},{9,11},{10,... | collective-permute-start | bytes 589832 | tf_op jit(solution)/shard_map/ppermute | solution.py:536
  22.1 0.2 collective-permute-start.10
  22.3 0.0 collective-permute-done.5.refs_2_
  22.3 0.0 collective-permute-done.6.refs_3_
  22.3 0.0 copy-done.1
  22.3 0.0 copy-done
  22.3 3.8 %shard_map.111.refs_1_ = f32[8,2,16,8,128]{4,3,2,1,0:T(8,128)S(1)} custom-call(f32[4,4,4096]{2,1,0:T(4,128)S(1)} %pad_maximum_fusion.refs_0_, f32[4,4,4096]{2,1,0:T(4,128)S(1)} %shard_map.110.refs_1_, f32[4,4,4096]{2,1,0:T(4,128)S(1)} %collective-permute-done.5.refs_2_, f32[4,4,4096]{2,1,0:T(4,128)S(1)} %collective-permute-done.6.refs_3_, ...), custom_call_target="tpu_custom_call" | custom-call | tf_op jit(solution)/shard_map/pallas_call | solution.py:498
  26.1 1.8 %collective-permute-done.8.refs_0_ = f32[3,4,4096]{2,1,0:T(4,128)S(1)} collective-permute-done((f32[3,4,4096]{2,1,0:T(4,128)S(1)}, f32[3,4,4096]{2,1,0:T(4,128)S(1)}, u32[]{:S(2)}, u32[]{:S(2)}) %collective-permute-start.8) | collective-permute-done | bytes 196640 | tf_op jit(solution)/shard_map/ppermute | solution.py:536
  27.9 0.0 collective-permute-start.9
  27.9 0.0 collective-permute-done.10.refs_2_
  27.9 2.7 %shard_map.113 = (f32[4,4,12,8,128]{4,3,2,1,0:T(8,128)S(1)}, f32[4,8,4096]{2,1,0:T(8,128)S(1)}) custom-call(f32[3,4,4096]{2,1,0:T(4,128)S(1)} %collective-permute-done.7.refs_0_, f32[3,4,4096]{2,1,0:T(4,128)S(1)} %shard_map.112.refs_1_, f32[3,4,4096]{2,1,0:T(4,128)} %collective-permute-done.10.refs_2_, f32[8,16384]{1,0:T(8,128)S(1)} %copy-done, ...), custom_call_target="tpu_custom_call" | custom-call | tf_op jit(solution)/shard_map/pallas_call | solution.py:498
  30.6 0.0 collective-permute-done.9.refs_0_
  30.6 0.0 copy-start.3
  30.6 2.1 %shard_map.114 = f32[8,2,12,8,128]{4,3,2,1,0:T(8,128)S(1)} custom-call(f32[3,4,4096]{2,1,0:T(4,128)S(1)} %collective-permute-done.9.refs_0_, f32[4,4,12,8,128]{4,3,2,1,0:T(8,128)S(1)} %get-tuple-element.7.refs_1_, f32[4,8,4096]{2,1,0:T(8,128)S(1)} %get-tuple-element.8.refs_2_, f32[8,32]{1,0:T(8,128)S(1)} %copy-done.6, f32[8,32]{1,0:T(8,128)S(1)} %copy-done.7, ...), custom_call_target="tpu_custom_call" | custom-call | tf_op jit(solution)/shard_map/pallas_call | solution.py:498
  32.7 0.0 copy-done.3
  32.7 0.0 copy-start.2
  32.7 2.9 %shard_map.115 = f32[256,128]{1,0:T(8,128)S(1)} custom-call(f32[1,8,2,4,8,128]{5,4,3,2,1,0:T(8,128)S(1)} %bitcast.12, f32[1,8,2,16,8,128]{5,4,3,2,1,0:T(8,128)S(1)} %bitcast.10, f32[1,8,2,12,8,128]{5,4,3,2,1,0:T(8,128)S(1)} %bitcast.11, bf16[768,128]{1,0:T(8,128)(2,1)S(1)} %copy-done.3), custom_call_target="tpu_custom_call" | custom-call | tf_op jit(solution)/shard_map/pallas_call | solution.py:498
  35.6 0.0 copy-start.4
  35.6 0.0 copy-start.5
  35.6 11.8 %all_to_all.11 = f32[32,8,128]{2,1,0:T(8,128)S(1)} all-to-all(f32[32,8,128]{2,1,0:T(8,128)S(1)} %bitcast.13), channel_id=1, replica_groups=mesh['comp'=8,'rank'=4] {'comp','rank'}, dimensions={0} | all-to-all | bytes 262144 | tf_op jit(solution)/shard_map/all_to_all | solution.py:639
  47.4 0.0 copy-done.2
  47.4 0.0 copy-done.4
  47.5 0.0 copy-done.5
  47.5 0.9 %shard_map.116 = f32[128,128]{1,0:T(8,128)} custom-call(f32[256,128]{1,0:T(8,128)S(1)} %bitcast.14, f32[256,128]{1,0:T(8,128)S(1)} %copy-done.5, f32[256,128]{1,0:T(8,128)S(1)} %copy-done.4, bf16[128,1536]{1,0:T(8,128)(2,1)S(1)} %copy-done.2), custom_call_target="tpu_custom_call" | custom-call | tf_op jit(solution)/shard_map/pallas_call | solution.py:498
  (3 shorter events, 0.0 us)
Async XLA Ops:
  0.8 7.6 %collective-permute-start.3 = (f32[4,4096]{1,0:T(4,128)S(1)}, f32[4,4096]{1,0:T(4,128)S(1)}, u32[]{:S(2)}, u32[]{:S(2)}) collective-permute-start(f32[4,4096]{1,0:T(4,128)S(1)} %constant_dynamic-slice_fusion), channel_id=1, source_target_pairs={{0,24},{4,28},{8,0},{12,4},{16,8},{20,12},{24,16},{28,20},{1,25},{... | collective-permute-start | bytes 196616 | tf_op jit(solution)/shard_map/ppermute | solution.py:530
  5.9 6.5 %collective-permute-start.2 = (f32[4,4096]{1,0:T(4,128)S(1)}, f32[4,4096]{1,0:T(4,128)S(1)}, u32[]{:S(2)}, u32[]{:S(2)}) collective-permute-start(f32[4,4096]{1,0:T(4,128)S(1)} %constant_dynamic-slice_fusion), channel_id=1, source_target_pairs={{0,16},{4,20},{8,24},{12,28},{16,0},{20,4},{24,8},{28,12},{1,17},{... | collective-permute-start | bytes 196616 | tf_op jit(solution)/shard_map/ppermute | solution.py:530
  5.9 6.5 %collective-permute-start.1 = (f32[4,4096]{1,0:T(4,128)S(1)}, f32[4,4096]{1,0:T(4,128)S(1)}, u32[]{:S(2)}, u32[]{:S(2)}) collective-permute-start(f32[4,4096]{1,0:T(4,128)S(1)} %constant_dynamic-slice_fusion), channel_id=1, source_target_pairs={{0,8},{4,12},{8,16},{12,20},{16,24},{20,28},{24,0},{28,4},{1,9},{5... | collective-permute-start | bytes 196616 | tf_op jit(solution)/shard_map/ppermute | solution.py:530
  6.9 5.5 %collective-permute-start = (f32[4,4096]{1,0:T(4,128)S(1)}, f32[4,4096]{1,0:T(4,128)S(1)}, u32[]{:S(2)}, u32[]{:S(2)}) collective-permute-start(f32[4,4096]{1,0:T(4,128)S(1)} %constant_dynamic-slice_fusion), channel_id=1, source_target_pairs={{0,4},{4,0},{8,12},{12,8},{16,20},{20,16},{24,28},{28,24},{1,5},{5... | collective-permute-start | bytes 196616 | tf_op jit(solution)/shard_map/ppermute | solution.py:533
  12.4 3.2 %copy-start.6 = (f32[8,32]{1,0:T(8,128)S(1)}, f32[8,32]{1,0:T(8,128)}, u32[]{:S(2)}) copy-start(f32[8,32]{1,0:T(8,128)} %refs_3_.4) | copy-start | bytes 3076
  12.4 3.2 %copy-start.7 = (f32[8,32]{1,0:T(8,128)S(1)}, f32[8,32]{1,0:T(8,128)}, u32[]{:S(2)}) copy-start(f32[8,32]{1,0:T(8,128)} %refs_4_.5) | copy-start | bytes 3076
  12.5 8.1 %collective-permute-start.4 = (f32[4,4,4096]{2,1,0:T(4,128)S(1)}, f32[4,4,4096]{2,1,0:T(4,128)S(1)}, u32[]{:S(2)}, u32[]{:S(2)}) collective-permute-start(f32[4,4,4096]{2,1,0:T(4,128)S(1)} %pad_maximum_fusion.refs_0_), channel_id=1, source_target_pairs={{0,2},{1,3},{2,0},{3,1},{4,6},{5,7},{6,4},{7,5},{8,10},{9,11},{10,... | collective-permute-start | bytes 786440 | tf_op jit(solution)/shard_map/ppermute | solution.py:536
  14.1 6.5 %collective-permute-start.7 = (f32[3,4,4096]{2,1,0:T(4,128)S(1)}, f32[3,4,4096]{2,1,0:T(4,128)S(1)}, u32[]{:S(2)}, u32[]{:S(2)}) collective-permute-start(f32[3,4,4096]{2,1,0:T(4,128)S(1)} %pad_maximum_fusion.1), channel_id=1, source_target_pairs={{0,4},{4,0},{8,12},{12,8},{16,20},{20,16},{24,28},{28,24},{1,5},{5... | collective-permute-start | bytes 589832 | tf_op jit(solution)/shard_map/ppermute | solution.py:533
  15.7 6.6 %collective-permute-start.5 = (f32[4,4,4096]{2,1,0:T(4,128)S(1)}, f32[4,4,4096]{2,1,0:T(4,128)S(1)}, u32[]{:S(2)}, u32[]{:S(2)}) collective-permute-start(f32[4,4,4096]{2,1,0:T(4,128)S(1)} %pad_maximum_fusion.refs_0_), channel_id=1, source_target_pairs={{0,1},{1,0},{2,3},{3,2},{4,5},{5,4},{6,7},{7,6},{8,9},{9,8},{10,11... | collective-permute-start | bytes 786440 | tf_op jit(solution)/shard_map/ppermute | solution.py:536
  15.7 6.6 %copy-start.1 = (f32[8,16384]{1,0:T(8,128)S(1)}, f32[8,16384]{1,0:T(8,128)}, u32[]{:S(2)}) copy-start(f32[8,16384]{1,0:T(8,128)} %refs_4_.4) | copy-start | bytes 1572868
  18.8 3.5 %copy-start = (f32[8,16384]{1,0:T(8,128)S(1)}, f32[8,16384]{1,0:T(8,128)}, u32[]{:S(2)}) copy-start(f32[8,16384]{1,0:T(8,128)} %refs_3_.3) | copy-start | bytes 1572868
  20.6 1.7 %collective-permute-start.6 = (f32[4,4,4096]{2,1,0:T(4,128)S(1)}, f32[4,4,4096]{2,1,0:T(4,128)S(1)}, u32[]{:S(2)}, u32[]{:S(2)}) collective-permute-start(f32[4,4,4096]{2,1,0:T(4,128)S(1)} %shard_map.110.refs_1_), channel_id=1, source_target_pairs={{0,1},{1,0},{2,3},{3,2},{4,5},{5,4},{6,7},{7,6},{8,9},{9,8},{10,11... | collective-permute-start | bytes 786440 | tf_op jit(solution)/shard_map/ppermute | solution.py:536
  20.6 7.3 %collective-permute-start.8 = (f32[3,4,4096]{2,1,0:T(4,128)S(1)}, f32[3,4,4096]{2,1,0:T(4,128)S(1)}, u32[]{:S(2)}, u32[]{:S(2)}) collective-permute-start(f32[3,4,4096]{2,1,0:T(4,128)S(1)} %collective-permute-done.7.refs_0_), channel_id=1, source_target_pairs={{0,2},{1,3},{2,0},{3,1},{4,6},{5,7},{6,4},{7,5},{8,10},{9,11},{10,... | collective-permute-start | bytes 589832 | tf_op jit(solution)/shard_map/ppermute | solution.py:536
  22.1 5.8 %collective-permute-start.10 = (f32[3,4,4096]{2,1,0:T(4,128)S(1)}, f32[3,4,4096]{2,1,0:T(4,128)}, u32[]{:S(2)}, u32[]{:S(2)}) collective-permute-start(f32[3,4,4096]{2,1,0:T(4,128)S(1)} %collective-permute-done.7.refs_0_), channel_id=1, source_target_pairs={{0,1},{1,0},{2,3},{3,2},{4,5},{5,4},{6,7},{7,6},{8,9},{9,8},{10,11... | collective-permute-start | bytes 589832 | tf_op jit(solution)/shard_map/ppermute | solution.py:536
  27.9 2.7 %collective-permute-start.9 = (f32[3,4,4096]{2,1,0:T(4,128)S(1)}, f32[3,4,4096]{2,1,0:T(4,128)S(1)}, u32[]{:S(2)}, u32[]{:S(2)}) collective-permute-start(f32[3,4,4096]{2,1,0:T(4,128)S(1)} %shard_map.112.refs_1_), channel_id=1, source_target_pairs={{0,1},{1,0},{2,3},{3,2},{4,5},{5,4},{6,7},{7,6},{8,9},{9,8},{10,11... | collective-permute-start | bytes 589832 | tf_op jit(solution)/shard_map/ppermute | solution.py:536
  30.6 2.1 %copy-start.3 = (bf16[768,128]{1,0:T(8,128)(2,1)S(1)}, bf16[768,128]{1,0:T(8,128)(2,1)}, u32[]{:S(2)}) copy-start(bf16[768,128]{1,0:T(8,128)(2,1)} %constant.38.refs_3_) | copy-start | bytes 589828
  32.7 14.7 %copy-start.2 = (bf16[128,1536]{1,0:T(8,128)(2,1)S(1)}, bf16[128,1536]{1,0:T(8,128)(2,1)}, u32[]{:S(2)}) copy-start(bf16[128,1536]{1,0:T(8,128)(2,1)} %constant.43.refs_3_) | copy-start | bytes 1179652
  35.6 11.9 %copy-start.4 = (f32[256,128]{1,0:T(8,128)S(1)}, f32[256,128]{1,0:T(8,128)}, u32[]{:S(2)}) copy-start(f32[256,128]{1,0:T(8,128)} %constant.26.clone.refs_2_) | copy-start | bytes 393220
  35.6 11.8 %copy-start.5 = (f32[256,128]{1,0:T(8,128)S(1)}, f32[256,128]{1,0:T(8,128)}, u32[]{:S(2)}) copy-start(f32[256,128]{1,0:T(8,128)} %constant.25.clone.refs_1_) | copy-start | bytes 393220

commit v2 on v0

--- a/solution.py
+++ b/solution.py
@@ -189,14 +189,23 @@
     width = phases.shape[1] * LANES
     device_at = lax.axis_index("comp") * lax.axis_size("rank") + lax.axis_index("rank")
     odd = 4 * lax.rem(device_at, groups) + 1
-    shape = phases.shape[1:]
-    cells = lax.broadcasted_iota(jnp.int32, shape, 0) * LANES
-    cells = cells + lax.broadcasted_iota(jnp.int32, shape, 1)
-    turns = (cells * odd) & (4 * width - 1)
-    turns = jnp.where(turns >= 2 * width, turns - 4 * width, turns)
-    angles = turns.astype(jnp.float32) * (2.0 * math.pi / (4 * width))
-    phases[0] = jnp.cos(angles)
-    phases[1] = -jnp.sin(angles)
+
+    def turned(cells):
+        turns = (cells * odd) & (4 * width - 1)
+        turns = jnp.where(turns >= 2 * width, turns - 4 * width, turns)
+        angles = turns.astype(jnp.float32) * (2.0 * math.pi / (4 * width))
+        return jnp.cos(angles), -jnp.sin(angles)
+
+    count = phases.shape[1] // 8
+    rows = lax.broadcasted_iota(jnp.int32, (8, LANES), 0)
+    fine_cos, fine_sin = turned(rows * LANES + lax.broadcasted_iota(jnp.int32, (8, LANES), 1))
+    rows = lax.broadcasted_iota(jnp.int32, (count, LANES), 0)
+    coarse_cos, coarse_sin = turned(rows * (8 * LANES))
+    for tile in range(count):
+        cosine = jnp.broadcast_to(coarse_cos[tile : tile + 1], (8, LANES))
+        sine = jnp.broadcast_to(coarse_sin[tile : tile + 1], (8, LANES))
+        phases[0, pl.ds(tile * 8, 8), :] = fine_cos * cosine - fine_sin * sine
+        phases[1, pl.ds(tile * 8, 8), :] = fine_cos * sine + fine_sin * cosine
 
 
 def made_factors(columns, phases, kept):
@@ -242,7 +251,7 @@
 
 
 def own_kernel(blocks, groups, sources, *refs):
-    row_factors, sent, refs = refs[0:2], refs[2:7], refs[7:]
+    row_factors, sent, refs = refs[1:3], refs[3:8], refs[8:]
     out, partial, joined, phases, weights = refs[:5]
     held, arrivals = refs[5:10], refs[10]
     copies = start_tables(sent, held, arrivals)
@@ -510,16 +519,13 @@
         return [(tuple((q, k) for q in range(4)), *place) for k, place in enumerate(places)]
 
     lined = [along(mine, step) for step in range(1, lines)]
-    flipped_own = across(mine)
-    own = spectra(own_kernel, [own_source], (), (*tables, density, *columns))
-    (lined[lines // 2 - 1],) = after([lined[lines // 2 - 1]], own)
-    near = jnp.stack([flipped_own, *lined])
+    near = jnp.stack([across(mine), *lined])
     flipped = across(jnp.stack(lined))
-    beyond = swapped(near, 2)
-    ready = [near, beyond, swapped(near, 1), swapped(beyond, 1)]
-    flipped_beyond = swapped(flipped, 2)
-    flipped_beside = swapped(flipped, 1)
-    first = joined_spectra(ready, quartered(early))
+    beyond, beside = swapped(near, 2), swapped(near, 1)
+    flipped_beyond, flipped_beside = swapped(flipped, 2), swapped(flipped, 1)
+    own = spectra(own_kernel, [own_source], (near,), (*tables, density, *columns))
+    (beyond,) = after([beyond], own)
+    first = joined_spectra([near, beyond, beside, swapped(beyond, 1)], quartered(early))
     (flipped_beyond,) = after([flipped_beyond], first)
     second = joined_spectra(
         [flipped, flipped_beyond, flipped_beside, swapped(flipped_beyond, 1)], quartered(late)

time: 47.6 us -> 48 us (level)
  starting transfers between devices: 13.5 us -> 12.3 us
  Pallas kernels: 13.6 us -> 14.3 us
  blocking collectives: 11.3 us -> 12 us
    ppermute x6, waiting for transfers between devices: 7.43 us -> 4.78 us  [swapped(): return lax.ppermute(block, 'rank', [(r, r ^ other) for r in range(ranks)])]
    ppermute x3, waiting for transfers between devices: 0.01 us -> 1.85 us  [along(): return lax.ppermute(block, 'comp', pairs)]
    ppermute x2, waiting for transfers between devices: 0.35 us -> 1.38 us  [across(): return lax.ppermute(block, 'comp', [(c, c ^ 1) for c in range(comps)])]
    ppermute x3, starting transfers between devices: 7.86 us -> 6.96 us  [along(): return lax.ppermute(block, 'comp', pairs)]
    pallas_call x5, Pallas kernels: 13.6 us -> 14.3 us  [whole_call(): pl.pallas_call(kernel, out_shape=[out_type(shape, jnp.float32) for shape...]
    all_to_all x1, blocking collectives: 11.3 us -> 12 us  [body(): spread = lax.all_to_all(sent, AXES, split_axis=0, concat_axis=0, tiled=True)]
    ppermute x6, starting transfers between devices: 2.94 us -> 2.28 us  [swapped(): return lax.ppermute(block, 'rank', [(r, r ^ other) for r in range(ranks)])]
  transfers between devices with their start and end apart: 11 -> 11, of which waited for: 4 -> 8; matrix products, arithmetic and copies ran while one was open for 0% -> 0% of each run, Pallas kernels for 14% -> 14%
where the time goes in v2:
time: 48 us; the launch traced here: 47.8 us
  Pallas kernels  14.3 us (30%)
  starting transfers between devices  12.3 us (26%)
  blocking collectives  12 us (25%)
  waiting for transfers between devices  8 us (17%)
  local copies, waits for them, and re-layouts  0.89 us (2%)
    pallas_call x5, Pallas kernels, whole_call(): pl.pallas_call(kernel, out_shape=[out_type(shape, jnp.float32) for shape...  14.3 us
    all_to_all x1, blocking collectives, body(): spread = lax.all_to_all(sent, AXES, split_axis=0, concat_axis=0, tiled=True)  12 us
    ppermute x3, starting transfers between devices, along(): return lax.ppermute(block, 'comp', pairs)  6.96 us
    ppermute x6, waiting for transfers between devices, swapped(): return lax.ppermute(block, 'rank', [(r, r ^ other) for r in range(ranks)])  4.78 us
    ppermute x2, starting transfers between devices, across(): return lax.ppermute(block, 'comp', [(c, c ^ 1) for c in range(comps)])  3.1 us
    ppermute x6, starting transfers between devices, swapped(): return lax.ppermute(block, 'rank', [(r, r ^ other) for r in range(ranks)])  2.28 us
    ppermute x3, waiting for transfers between devices, along(): return lax.ppermute(block, 'comp', pairs)  1.85 us
    ppermute x2, waiting for transfers between devices, across(): return lax.ppermute(block, 'comp', [(c, c ^ 1) for c in range(comps)])  1.38 us
  transfers between devices with their start and end apart: 11, of which 8 were waited for; matrix products, arithmetic and copies ran while one was open for 0% of the time, Pallas kernels for 14%

profile of v2, /device:TPU:0, one launch (start us, length us, event | category | flops | bytes accessed | tf_op | source)
XLA Modules:
  0.0 47.8 jit_solution(12143302591705137433)
XLA Ops:
  0.0 0.8 %constant_dynamic-slice_fusion = f32[4,4096]{1,0:T(4,128)S(1)} fusion(f32[4,16384]{1,0:T(4,128)} %refs_5_.3, s32[]{:T(128)S(6)} %select_n.3), kind=kLoop, calls=%fused_computation.2 | loop fusion | bytes 131076 | tf_op jit(solution)/shard_map/dynamic_slice | solution.py:485
  0.8 3.0 %collective-permute-start.1 = (f32[4,4096]{1,0:T(4,128)S(1)}, f32[4,4096]{1,0:T(4,128)S(1)}, u32[]{:S(2)}, u32[]{:S(2)}) collective-permute-start(f32[4,4096]{1,0:T(4,128)S(1)} %constant_dynamic-slice_fusion), channel_id=1, source_target_pairs={{0,8},{4,12},{8,16},{12,20},{16,24},{20,28},{24,0},{28,4},{1,9},{5... | collective-permute-start | bytes 196616 | tf_op jit(solution)/shard_map/ppermute | solution.py:489
  3.9 2.6 %collective-permute-start.2 = (f32[4,4096]{1,0:T(4,128)S(1)}, f32[4,4096]{1,0:T(4,128)S(1)}, u32[]{:S(2)}, u32[]{:S(2)}) collective-permute-start(f32[4,4096]{1,0:T(4,128)S(1)} %constant_dynamic-slice_fusion), channel_id=1, source_target_pairs={{0,16},{4,20},{8,24},{12,28},{16,0},{20,4},{24,8},{28,12},{1,17},{... | collective-permute-start | bytes 196616 | tf_op jit(solution)/shard_map/ppermute | solution.py:489
  6.5 1.3 %collective-permute-start.3 = (f32[4,4096]{1,0:T(4,128)S(1)}, f32[4,4096]{1,0:T(4,128)S(1)}, u32[]{:S(2)}, u32[]{:S(2)}) collective-permute-start(f32[4,4096]{1,0:T(4,128)S(1)} %constant_dynamic-slice_fusion), channel_id=1, source_target_pairs={{0,24},{4,28},{8,0},{12,4},{16,8},{20,12},{24,16},{28,20},{1,25},{... | collective-permute-start | bytes 196616 | tf_op jit(solution)/shard_map/ppermute | solution.py:489
  7.8 1.5 %collective-permute-start = (f32[4,4096]{1,0:T(4,128)S(1)}, f32[4,4096]{1,0:T(4,128)S(1)}, u32[]{:S(2)}, u32[]{:S(2)}) collective-permute-start(f32[4,4096]{1,0:T(4,128)S(1)} %constant_dynamic-slice_fusion), channel_id=1, source_target_pairs={{0,4},{4,0},{8,12},{12,8},{16,20},{20,16},{24,28},{28,24},{1,5},{5... | collective-permute-start | bytes 196616 | tf_op jit(solution)/shard_map/ppermute | solution.py:492
  9.3 0.0 collective-permute-done.1
  9.3 1.6 %collective-permute-done.2 = f32[4,4096]{1,0:T(4,128)S(1)} collective-permute-done((f32[4,4096]{1,0:T(4,128)S(1)}, f32[4,4096]{1,0:T(4,128)S(1)}, u32[]{:S(2)}, u32[]{:S(2)}) %collective-permute-start.2) | collective-permute-done | bytes 65568 | tf_op jit(solution)/shard_map/ppermute | solution.py:489
  10.9 0.2 collective-permute-done.3
  11.2 0.9 %collective-permute-done = f32[4,4096]{1,0:T(4,128)S(1)} collective-permute-done((f32[4,4096]{1,0:T(4,128)S(1)}, f32[4,4096]{1,0:T(4,128)S(1)}, u32[]{:S(2)}, u32[]{:S(2)}) %collective-permute-start) | collective-permute-done | bytes 65568 | tf_op jit(solution)/shard_map/ppermute | solution.py:492
  12.1 0.1 pad_maximum_fusion.refs_0_
  12.1 0.0 copy-start.6
  12.2 0.0 copy-start.7
  12.2 1.6 %collective-permute-start.4 = (f32[4,4,4096]{2,1,0:T(4,128)S(1)}, f32[4,4,4096]{2,1,0:T(4,128)S(1)}, u32[]{:S(2)}, u32[]{:S(2)}) collective-permute-start(f32[4,4,4096]{2,1,0:T(4,128)S(1)} %pad_maximum_fusion.refs_0_), channel_id=1, source_target_pairs={{0,2},{1,3},{2,0},{3,1},{4,6},{5,7},{6,4},{7,5},{8,10},{9,11},{10,... | collective-permute-start | bytes 786440 | tf_op jit(solution)/shard_map/ppermute | solution.py:495
  13.8 1.6 %collective-permute-start.7 = (f32[3,4,4096]{2,1,0:T(4,128)S(1)}, f32[3,4,4096]{2,1,0:T(4,128)}, u32[]{:S(2)}, u32[]{:S(2)}) collective-permute-start(f32[3,4,4096]{2,1,0:T(4,128)S(1)} %pad_maximum_fusion.1), channel_id=1, source_target_pairs={{0,4},{4,0},{8,12},{12,8},{16,20},{20,16},{24,28},{28,24},{1,5},{5... | collective-permute-start | bytes 589832 | tf_op jit(solution)/shard_map/ppermute | solution.py:492
  15.4 0.0 collective-permute-start.5
  15.4 0.0 copy-done.6
  15.4 0.0 copy-done.7
  15.4 0.0 copy-start.1
  15.4 3.1 %shard_map.109.refs_1_ = f32[8,2,4,8,128]{4,3,2,1,0:T(8,128)S(1)} custom-call(f32[4,4,4096]{2,1,0:T(4,128)S(1)} %pad_maximum_fusion.refs_0_, f32[8,32]{1,0:T(8,128)S(1)} %copy-done.6, f32[8,32]{1,0:T(8,128)S(1)} %copy-done.7, f32[4,2,8,128]{3,2,1,0:T(8,128)} %constant.22.clone.refs_3_.refs_8_, bf16[768,256]{1,0:T(8,128)(2,1)} %constant.33.refs_4_.refs_9_, ...), custom_call_target="tpu_custom_call" | custom-call | tf_op jit(solution)/shard_map/pallas_call | solution.py:457
  18.5 0.0 copy-start
  18.5 0.6 %collective-permute-done.4.refs_0_ = f32[4,4,4096]{2,1,0:T(4,128)S(1)} collective-permute-done((f32[4,4,4096]{2,1,0:T(4,128)S(1)}, f32[4,4,4096]{2,1,0:T(4,128)S(1)}, u32[]{:S(2)}, u32[]{:S(2)}) %collective-permute-start.4) | collective-permute-done | bytes 262176 | tf_op jit(solution)/shard_map/ppermute | solution.py:495
  19.1 0.0 collective-permute-start.6
  19.1 0.5 collective-permute-done.7.refs_0_
  19.6 0.5 %collective-permute-start.8 = (f32[3,4,4096]{2,1,0:T(4,128)}, f32[3,4,4096]{2,1,0:T(4,128)S(1)}, u32[]{:S(2)}, u32[]{:S(2)}) collective-permute-start(f32[3,4,4096]{2,1,0:T(4,128)} %collective-permute-done.7.refs_0_), channel_id=1, source_target_pairs={{0,2},{1,3},{2,0},{3,1},{4,6},{5,7},{6,4},{7,5},{8,10},{9,11},{10,... | collective-permute-start | bytes 589832 | tf_op jit(solution)/shard_map/ppermute | solution.py:495
  20.2 0.2 collective-permute-start.9
  20.3 0.0 collective-permute-done.5.refs_2_
  20.3 0.3 collective-permute-done.6.refs_3_
  20.7 0.0 copy-done.1
  20.7 0.0 copy-done
  20.7 3.6 %shard_map.111.refs_1_ = f32[8,2,16,8,128]{4,3,2,1,0:T(8,128)S(1)} custom-call(f32[4,4,4096]{2,1,0:T(4,128)S(1)} %pad_maximum_fusion.refs_0_, f32[4,4,4096]{2,1,0:T(4,128)S(1)} %shard_map.110.refs_1_, f32[4,4,4096]{2,1,0:T(4,128)S(1)} %collective-permute-done.5.refs_2_, f32[4,4,4096]{2,1,0:T(4,128)S(1)} %collective-permute-done.6.refs_3_, ...), custom_call_target="tpu_custom_call" | custom-call | tf_op jit(solution)/shard_map/pallas_call | solution.py:457
  24.3 2.4 %collective-permute-done.8.refs_0_ = f32[3,4,4096]{2,1,0:T(4,128)S(1)} collective-permute-done((f32[3,4,4096]{2,1,0:T(4,128)}, f32[3,4,4096]{2,1,0:T(4,128)S(1)}, u32[]{:S(2)}, u32[]{:S(2)}) %collective-permute-start.8) | collective-permute-done | bytes 196640 | tf_op jit(solution)/shard_map/ppermute | solution.py:495
  26.7 0.0 copy-start.3
  26.7 0.0 collective-permute-start.10
  26.7 0.0 collective-permute-done.9.refs_2_
  26.7 1.4 %collective-permute-done.10.refs_3_ = f32[3,4,4096]{2,1,0:T(4,128)S(1)} collective-permute-done((f32[3,4,4096]{2,1,0:T(4,128)S(1)}, f32[3,4,4096]{2,1,0:T(4,128)S(1)}, u32[]{:S(2)}, u32[]{:S(2)}) %collective-permute-start.10) | collective-permute-done | bytes 196640 | tf_op jit(solution)/shard_map/ppermute | solution.py:495
  28.1 3.9 %shard_map.113 = f32[8,2,12,8,128]{4,3,2,1,0:T(8,128)S(1)} custom-call(f32[3,4,4096]{2,1,0:T(4,128)} %collective-permute-done.7.refs_0_, f32[3,4,4096]{2,1,0:T(4,128)S(1)} %shard_map.112.refs_1_, f32[3,4,4096]{2,1,0:T(4,128)} %collective-permute-done.9.refs_2_, f32[3,4,4096]{2,1,0:T(4,128)S(1)} %collective-permute-done.10.refs_3_, f32[8,16384]{1,0:T(8,128)S(1)} %copy-done, ...), custom_call_target="tpu_custom_call" | custom-call | tf_op jit(solution)/shard_map/pallas_call | solution.py:457
  32.0 0.0 copy-done.3
  32.0 0.0 copy-start.2
  32.0 2.9 %shard_map.114 = f32[256,128]{1,0:T(8,128)S(1)} custom-call(f32[1,8,2,4,8,128]{5,4,3,2,1,0:T(8,128)S(1)} %bitcast.12, f32[1,8,2,16,8,128]{5,4,3,2,1,0:T(8,128)S(1)} %bitcast.10, f32[1,8,2,12,8,128]{5,4,3,2,1,0:T(8,128)S(1)} %bitcast.11, bf16[768,128]{1,0:T(8,128)(2,1)S(1)} %copy-done.3), custom_call_target="tpu_custom_call" | custom-call | tf_op jit(solution)/shard_map/pallas_call | solution.py:457
  34.9 0.0 copy-start.4
  34.9 0.0 copy-start.5
  34.9 12.0 %all_to_all.11 = f32[32,8,128]{2,1,0:T(8,128)S(1)} all-to-all(f32[32,8,128]{2,1,0:T(8,128)S(1)} %bitcast.13), channel_id=1, replica_groups=mesh['comp'=8,'rank'=4] {'comp','rank'}, dimensions={0} | all-to-all | bytes 262144 | tf_op jit(solution)/shard_map/all_to_all | solution.py:592
  46.9 0.0 copy-done.2
  46.9 0.0 copy-done.4
  46.9 0.0 copy-done.5
  46.9 0.9 %shard_map.115 = f32[128,128]{1,0:T(8,128)} custom-call(f32[256,128]{1,0:T(8,128)S(1)} %bitcast.14, f32[256,128]{1,0:T(8,128)S(1)} %copy-done.4, f32[256,128]{1,0:T(8,128)S(1)} %copy-done.5, bf16[128,1536]{1,0:T(8,128)(2,1)S(1)} %copy-done.2), custom_call_target="tpu_custom_call" | custom-call | tf_op jit(solution)/shard_map/pallas_call | solution.py:457
  (3 shorter events, 0.0 us)
Async XLA Ops:
  0.8 8.5 %collective-permute-start.1 = (f32[4,4096]{1,0:T(4,128)S(1)}, f32[4,4096]{1,0:T(4,128)S(1)}, u32[]{:S(2)}, u32[]{:S(2)}) collective-permute-start(f32[4,4096]{1,0:T(4,128)S(1)} %constant_dynamic-slice_fusion), channel_id=1, source_target_pairs={{0,8},{4,12},{8,16},{12,20},{16,24},{20,28},{24,0},{28,4},{1,9},{5... | collective-permute-start | bytes 196616 | tf_op jit(solution)/shard_map/ppermute | solution.py:489
  3.9 7.1 %collective-permute-start.2 = (f32[4,4096]{1,0:T(4,128)S(1)}, f32[4,4096]{1,0:T(4,128)S(1)}, u32[]{:S(2)}, u32[]{:S(2)}) collective-permute-start(f32[4,4096]{1,0:T(4,128)S(1)} %constant_dynamic-slice_fusion), channel_id=1, source_target_pairs={{0,16},{4,20},{8,24},{12,28},{16,0},{20,4},{24,8},{28,12},{1,17},{... | collective-permute-start | bytes 196616 | tf_op jit(solution)/shard_map/ppermute | solution.py:489
  6.5 4.7 %collective-permute-start.3 = (f32[4,4096]{1,0:T(4,128)S(1)}, f32[4,4096]{1,0:T(4,128)S(1)}, u32[]{:S(2)}, u32[]{:S(2)}) collective-permute-start(f32[4,4096]{1,0:T(4,128)S(1)} %constant_dynamic-slice_fusion), channel_id=1, source_target_pairs={{0,24},{4,28},{8,0},{12,4},{16,8},{20,12},{24,16},{28,20},{1,25},{... | collective-permute-start | bytes 196616 | tf_op jit(solution)/shard_map/ppermute | solution.py:489
  7.8 4.3 %collective-permute-start = (f32[4,4096]{1,0:T(4,128)S(1)}, f32[4,4096]{1,0:T(4,128)S(1)}, u32[]{:S(2)}, u32[]{:S(2)}) collective-permute-start(f32[4,4096]{1,0:T(4,128)S(1)} %constant_dynamic-slice_fusion), channel_id=1, source_target_pairs={{0,4},{4,0},{8,12},{12,8},{16,20},{20,16},{24,28},{28,24},{1,5},{5... | collective-permute-start | bytes 196616 | tf_op jit(solution)/shard_map/ppermute | solution.py:492
  12.1 3.2 %copy-start.6 = (f32[8,32]{1,0:T(8,128)S(1)}, f32[8,32]{1,0:T(8,128)}, u32[]{:S(2)}) copy-start(f32[8,32]{1,0:T(8,128)} %refs_6_.5) | copy-start | bytes 3076
  12.2 3.2 %copy-start.7 = (f32[8,32]{1,0:T(8,128)S(1)}, f32[8,32]{1,0:T(8,128)}, u32[]{:S(2)}) copy-start(f32[8,32]{1,0:T(8,128)} %refs_7_.5) | copy-start | bytes 3076
  12.2 7.0 %collective-permute-start.4 = (f32[4,4,4096]{2,1,0:T(4,128)S(1)}, f32[4,4,4096]{2,1,0:T(4,128)S(1)}, u32[]{:S(2)}, u32[]{:S(2)}) collective-permute-start(f32[4,4,4096]{2,1,0:T(4,128)S(1)} %pad_maximum_fusion.refs_0_), channel_id=1, source_target_pairs={{0,2},{1,3},{2,0},{3,1},{4,6},{5,7},{6,4},{7,5},{8,10},{9,11},{10,... | collective-permute-start | bytes 786440 | tf_op jit(solution)/shard_map/ppermute | solution.py:495
  13.8 5.8 %collective-permute-start.7 = (f32[3,4,4096]{2,1,0:T(4,128)S(1)}, f32[3,4,4096]{2,1,0:T(4,128)}, u32[]{:S(2)}, u32[]{:S(2)}) collective-permute-start(f32[3,4,4096]{2,1,0:T(4,128)S(1)} %pad_maximum_fusion.1), channel_id=1, source_target_pairs={{0,4},{4,0},{8,12},{12,8},{16,20},{20,16},{24,28},{28,24},{1,5},{5... | collective-permute-start | bytes 589832 | tf_op jit(solution)/shard_map/ppermute | solution.py:492
  15.4 5.0 %collective-permute-start.5 = (f32[4,4,4096]{2,1,0:T(4,128)S(1)}, f32[4,4,4096]{2,1,0:T(4,128)S(1)}, u32[]{:S(2)}, u32[]{:S(2)}) collective-permute-start(f32[4,4,4096]{2,1,0:T(4,128)S(1)} %pad_maximum_fusion.refs_0_), channel_id=1, source_target_pairs={{0,1},{1,0},{2,3},{3,2},{4,5},{5,4},{6,7},{7,6},{8,9},{9,8},{10,11... | collective-permute-start | bytes 786440 | tf_op jit(solution)/shard_map/ppermute | solution.py:495
  15.4 5.3 %copy-start.1 = (f32[8,16384]{1,0:T(8,128)S(1)}, f32[8,16384]{1,0:T(8,128)}, u32[]{:S(2)}) copy-start(f32[8,16384]{1,0:T(8,128)} %refs_5_.5) | copy-start | bytes 1572868
  18.5 2.2 %copy-start = (f32[8,16384]{1,0:T(8,128)S(1)}, f32[8,16384]{1,0:T(8,128)}, u32[]{:S(2)}) copy-start(f32[8,16384]{1,0:T(8,128)} %refs_4_.3) | copy-start | bytes 1572868
  19.1 1.5 %collective-permute-start.6 = (f32[4,4,4096]{2,1,0:T(4,128)S(1)}, f32[4,4,4096]{2,1,0:T(4,128)S(1)}, u32[]{:S(2)}, u32[]{:S(2)}) collective-permute-start(f32[4,4,4096]{2,1,0:T(4,128)S(1)} %shard_map.110.refs_1_), channel_id=1, source_target_pairs={{0,1},{1,0},{2,3},{3,2},{4,5},{5,4},{6,7},{7,6},{8,9},{9,8},{10,11... | collective-permute-start | bytes 786440 | tf_op jit(solution)/shard_map/ppermute | solution.py:495
  19.6 7.1 %collective-permute-start.8 = (f32[3,4,4096]{2,1,0:T(4,128)}, f32[3,4,4096]{2,1,0:T(4,128)S(1)}, u32[]{:S(2)}, u32[]{:S(2)}) collective-permute-start(f32[3,4,4096]{2,1,0:T(4,128)} %collective-permute-done.7.refs_0_), channel_id=1, source_target_pairs={{0,2},{1,3},{2,0},{3,1},{4,6},{5,7},{6,4},{7,5},{8,10},{9,11},{10,... | collective-permute-start | bytes 589832 | tf_op jit(solution)/shard_map/ppermute | solution.py:495
  20.2 6.5 %collective-permute-start.9 = (f32[3,4,4096]{2,1,0:T(4,128)}, f32[3,4,4096]{2,1,0:T(4,128)}, u32[]{:S(2)}, u32[]{:S(2)}) collective-permute-start(f32[3,4,4096]{2,1,0:T(4,128)} %collective-permute-done.7.refs_0_), channel_id=1, source_target_pairs={{0,1},{1,0},{2,3},{3,2},{4,5},{5,4},{6,7},{7,6},{8,9},{9,8},{10,11... | collective-permute-start | bytes 589832 | tf_op jit(solution)/shard_map/ppermute | solution.py:495
  26.7 5.3 %copy-start.3 = (bf16[768,128]{1,0:T(8,128)(2,1)S(1)}, bf16[768,128]{1,0:T(8,128)(2,1)}, u32[]{:S(2)}) copy-start(bf16[768,128]{1,0:T(8,128)(2,1)} %constant.38.refs_3_) | copy-start | bytes 589828
  26.7 1.4 %collective-permute-start.10 = (f32[3,4,4096]{2,1,0:T(4,128)S(1)}, f32[3,4,4096]{2,1,0:T(4,128)S(1)}, u32[]{:S(2)}, u32[]{:S(2)}) collective-permute-start(f32[3,4,4096]{2,1,0:T(4,128)S(1)} %shard_map.112.refs_1_), channel_id=1, source_target_pairs={{0,1},{1,0},{2,3},{3,2},{4,5},{5,4},{6,7},{7,6},{8,9},{9,8},{10,11... | collective-permute-start | bytes 589832 | tf_op jit(solution)/shard_map/ppermute | solution.py:495
  32.0 14.9 %copy-start.2 = (bf16[128,1536]{1,0:T(8,128)(2,1)S(1)}, bf16[128,1536]{1,0:T(8,128)(2,1)}, u32[]{:S(2)}) copy-start(bf16[128,1536]{1,0:T(8,128)(2,1)} %constant.43.refs_3_) | copy-start | bytes 1179652
  34.9 12.0 %copy-start.4 = (f32[256,128]{1,0:T(8,128)S(1)}, f32[256,128]{1,0:T(8,128)}, u32[]{:S(2)}) copy-start(f32[256,128]{1,0:T(8,128)} %constant.25.clone.refs_1_) | copy-start | bytes 393220
  34.9 12.0 %copy-start.5 = (f32[256,128]{1,0:T(8,128)S(1)}, f32[256,128]{1,0:T(8,128)}, u32[]{:S(2)}) copy-start(f32[256,128]{1,0:T(8,128)} %constant.26.clone.refs_2_) | copy-start | bytes 393220

commit v3 on v2

--- a/solution.py
+++ b/solution.py
@@ -251,7 +251,7 @@
 
 
 def own_kernel(blocks, groups, sources, *refs):
-    row_factors, sent, refs = refs[1:3], refs[3:8], refs[8:]
+    row_factors, sent, refs = refs[0:2], refs[2:7], refs[7:]
     out, partial, joined, phases, weights = refs[:5]
     held, arrivals = refs[5:10], refs[10]
     copies = start_tables(sent, held, arrivals)
@@ -519,13 +519,16 @@
         return [(tuple((q, k) for q in range(4)), *place) for k, place in enumerate(places)]
 
     lined = [along(mine, step) for step in range(1, lines)]
-    near = jnp.stack([across(mine), *lined])
+    flipped_own = across(mine)
+    own = spectra(own_kernel, [own_source], (), (*tables, density, *columns))
+    (lined[lines // 2 - 1],) = after([lined[lines // 2 - 1]], own)
+    near = jnp.stack([flipped_own, *lined])
     flipped = across(jnp.stack(lined))
-    beyond, beside = swapped(near, 2), swapped(near, 1)
-    flipped_beyond, flipped_beside = swapped(flipped, 2), swapped(flipped, 1)
-    own = spectra(own_kernel, [own_source], (near,), (*tables, density, *columns))
-    (beyond,) = after([beyond], own)
-    first = joined_spectra([near, beyond, beside, swapped(beyond, 1)], quartered(early))
+    beyond = swapped(near, 2)
+    ready = [near, beyond, swapped(near, 1), swapped(beyond, 1)]
+    flipped_beyond = swapped(flipped, 2)
+    flipped_beside = swapped(flipped, 1)
+    first = joined_spectra(ready, quartered(early))
     (flipped_beyond,) = after([flipped_beyond], first)
     second = joined_spectra(
         [flipped, flipped_beyond, flipped_beside, swapped(flipped_beyond, 1)], quartered(late)

time: 48 us -> 47.4 us (0.987)
  starting transfers between devices: 12.3 us -> 13.5 us
  Pallas kernels: 14.3 us -> 13.3 us
  blocking collectives: 12 us -> 11.3 us
    ppermute x6, waiting for transfers between devices: 4.78 us -> 7.6 us  [swapped(): return lax.ppermute(block, 'rank', [(r, r ^ other) for r in range(ranks)])]
    ppermute x3, waiting for transfers between devices: 1.85 us -> 0.01 us  [along(): return lax.ppermute(block, 'comp', pairs)]
    pallas_call x5, Pallas kernels: 14.3 us -> 13.3 us  [whole_call(): pl.pallas_call(kernel, out_shape=[out_type(shape, jnp.float32) for shape...]
    ppermute x2, waiting for transfers between devices: 1.38 us -> 0.35 us  [across(): return lax.ppermute(block, 'comp', [(c, c ^ 1) for c in range(comps)])]
    ppermute x3, starting transfers between devices: 6.96 us -> 7.86 us  [along(): return lax.ppermute(block, 'comp', pairs)]
    all_to_all x1, blocking collectives: 12 us -> 11.3 us  [body(): spread = lax.all_to_all(sent, AXES, split_axis=0, concat_axis=0, tiled=True)]
    ppermute x6, starting transfers between devices: 2.28 us -> 2.94 us  [swapped(): return lax.ppermute(block, 'rank', [(r, r ^ other) for r in range(ranks)])]
  transfers between devices with their start and end apart: 11 -> 11, of which waited for: 8 -> 4; matrix products, arithmetic and copies ran while one was open for 0% -> 0% of each run, Pallas kernels for 14% -> 14%
where the time goes in v3:
time: 47.4 us; the launch traced here: 47.2 us
  starting transfers between devices  13.5 us (28%)
  Pallas kernels  13.3 us (28%)
  blocking collectives  11.3 us (24%)
  waiting for transfers between devices  7.96 us (17%)
  local copies, waits for them, and re-layouts  0.92 us (2%)
    pallas_call x5, Pallas kernels, whole_call(): pl.pallas_call(kernel, out_shape=[out_type(shape, jnp.float32) for shape...  13.3 us
    all_to_all x1, blocking collectives, body(): spread = lax.all_to_all(sent, AXES, split_axis=0, concat_axis=0, tiled=True)  11.3 us
    ppermute x3, starting transfers between devices, along(): return lax.ppermute(block, 'comp', pairs)  7.86 us
    ppermute x6, waiting for transfers between devices, swapped(): return lax.ppermute(block, 'rank', [(r, r ^ other) for r in range(ranks)])  7.6 us
    ppermute x6, starting transfers between devices, swapped(): return lax.ppermute(block, 'rank', [(r, r ^ other) for r in range(ranks)])  2.94 us
    ppermute x2, starting transfers between devices, across(): return lax.ppermute(block, 'comp', [(c, c ^ 1) for c in range(comps)])  2.7 us
  transfers between devices with their start and end apart: 11, of which 4 were waited for; matrix products, arithmetic and copies ran while one was open for 0% of the time, Pallas kernels for 14%

profile of v3, /device:TPU:0, one launch (start us, length us, event | category | flops | bytes accessed | tf_op | source)
XLA Modules:
  0.0 47.2 jit_solution(1115168918878692481)
XLA Ops:
  0.0 0.0 copy-start.6
  0.0 0.0 copy-start.7
  0.0 0.9 %constant_dynamic-slice_fusion = f32[4,4096]{1,0:T(4,128)S(1)} fusion(f32[4,16384]{1,0:T(4,128)} %refs_4_.3, s32[]{:T(128)S(6)} %select_n.3), kind=kLoop, calls=%fused_computation.2 | loop fusion | bytes 131076 | tf_op jit(solution)/shard_map/dynamic_slice | solution.py:485
  0.9 4.0 %collective-permute-start.2 = (f32[4,4096]{1,0:T(4,128)S(1)}, f32[4,4096]{1,0:T(4,128)S(1)}, u32[]{:S(2)}, u32[]{:S(2)}) collective-permute-start(f32[4,4096]{1,0:T(4,128)S(1)} %constant_dynamic-slice_fusion), channel_id=1, source_target_pairs={{0,16},{4,20},{8,24},{12,28},{16,0},{20,4},{24,8},{28,12},{1,17},{... | collective-permute-start | bytes 196616 | tf_op jit(solution)/shard_map/ppermute | solution.py:489
  4.9 1.6 %collective-permute-start.1 = (f32[4,4096]{1,0:T(4,128)S(1)}, f32[4,4096]{1,0:T(4,128)S(1)}, u32[]{:S(2)}, u32[]{:S(2)}) collective-permute-start(f32[4,4096]{1,0:T(4,128)S(1)} %constant_dynamic-slice_fusion), channel_id=1, source_target_pairs={{0,8},{4,12},{8,16},{12,20},{16,24},{20,28},{24,0},{28,4},{1,9},{5... | collective-permute-start | bytes 196616 | tf_op jit(solution)/shard_map/ppermute | solution.py:489
  6.5 2.2 %collective-permute-start.3 = (f32[4,4096]{1,0:T(4,128)S(1)}, f32[4,4096]{1,0:T(4,128)S(1)}, u32[]{:S(2)}, u32[]{:S(2)}) collective-permute-start(f32[4,4096]{1,0:T(4,128)S(1)} %constant_dynamic-slice_fusion), channel_id=1, source_target_pairs={{0,24},{4,28},{8,0},{12,4},{16,8},{20,12},{24,16},{28,20},{1,25},{... | collective-permute-start | bytes 196616 | tf_op jit(solution)/shard_map/ppermute | solution.py:489
  8.7 1.5 %collective-permute-start = (f32[4,4096]{1,0:T(4,128)S(1)}, f32[4,4096]{1,0:T(4,128)S(1)}, u32[]{:S(2)}, u32[]{:S(2)}) collective-permute-start(f32[4,4096]{1,0:T(4,128)S(1)} %constant_dynamic-slice_fusion), channel_id=1, source_target_pairs={{0,4},{4,0},{8,12},{12,8},{16,20},{20,16},{24,28},{28,24},{1,5},{5... | collective-permute-start | bytes 196616 | tf_op jit(solution)/shard_map/ppermute | solution.py:492
  10.3 0.0 copy-done.6
  10.3 0.0 copy-done.7
  10.3 3.1 %shard_map.109.refs_1_ = f32[8,2,4,8,128]{4,3,2,1,0:T(8,128)S(1)} custom-call(f32[8,32]{1,0:T(8,128)S(1)} %copy-done.6, f32[8,32]{1,0:T(8,128)S(1)} %copy-done.7, f32[4,2,8,128]{3,2,1,0:T(8,128)} %constant.22.clone.refs_2_.refs_8_, bf16[768,256]{1,0:T(8,128)(2,1)} %constant.33.refs_3_.refs_9_, f32[4,16384]{1,0:T(4,128)} %refs_4_.3, f32[8,16384]{1,0:T(8,128)} %refs_4_.5, ...), custom_call_target="tpu_custom_call" | custom-call | tf_op jit(solution)/shard_map/pallas_call | solution.py:457
  13.3 0.0 collective-permute-done.2.refs_0_
  13.3 0.0 copy-start.1
  13.4 0.0 copy-start
  13.4 0.0 collective-permute-done.1
  13.4 0.0 collective-permute-done.3
  13.4 0.0 collective-permute-done
  13.4 0.1 pad_maximum_fusion.refs_0_
  13.5 1.6 %collective-permute-start.4 = (f32[4,4,4096]{2,1,0:T(4,128)S(1)}, f32[4,4,4096]{2,1,0:T(4,128)S(1)}, u32[]{:S(2)}, u32[]{:S(2)}) collective-permute-start(f32[4,4,4096]{2,1,0:T(4,128)S(1)} %pad_maximum_fusion.refs_0_), channel_id=1, source_target_pairs={{0,2},{1,3},{2,0},{3,1},{4,6},{5,7},{6,4},{7,5},{8,10},{9,11},{10,... | collective-permute-start | bytes 786440 | tf_op jit(solution)/shard_map/ppermute | solution.py:495
  15.1 1.2 %collective-permute-start.7 = (f32[3,4,4096]{2,1,0:T(4,128)S(1)}, f32[3,4,4096]{2,1,0:T(4,128)S(1)}, u32[]{:S(2)}, u32[]{:S(2)}) collective-permute-start(f32[3,4,4096]{2,1,0:T(4,128)S(1)} %pad_maximum_fusion.1), channel_id=1, source_target_pairs={{0,4},{4,0},{8,12},{12,8},{16,20},{20,16},{24,28},{28,24},{1,5},{5... | collective-permute-start | bytes 589832 | tf_op jit(solution)/shard_map/ppermute | solution.py:492
  16.3 0.0 collective-permute-start.5
  16.3 4.2 %collective-permute-done.4.refs_1_ = f32[4,4,4096]{2,1,0:T(4,128)S(1)} collective-permute-done((f32[4,4,4096]{2,1,0:T(4,128)S(1)}, f32[4,4,4096]{2,1,0:T(4,128)S(1)}, u32[]{:S(2)}, u32[]{:S(2)}) %collective-permute-start.4) | collective-permute-done | bytes 262176 | tf_op jit(solution)/shard_map/ppermute | solution.py:495
  20.5 0.0 collective-permute-start.6
  20.5 0.3 collective-permute-done.7.refs_0_
  20.8 1.1 %collective-permute-start.8 = (f32[3,4,4096]{2,1,0:T(4,128)S(1)}, f32[3,4,4096]{2,1,0:T(4,128)S(1)}, u32[]{:S(2)}, u32[]{:S(2)}) collective-permute-start(f32[3,4,4096]{2,1,0:T(4,128)S(1)} %collective-permute-done.7.refs_0_), channel_id=1, source_target_pairs={{0,2},{1,3},{2,0},{3,1},{4,6},{5,7},{6,4},{7,5},{8,10},{9,11},{10,... | collective-permute-start | bytes 589832 | tf_op jit(solution)/shard_map/ppermute | solution.py:495
  22.0 0.2 collective-permute-start.9
  22.2 0.0 collective-permute-done.5.refs_2_
  22.2 0.0 collective-permute-done.6.refs_3_
  22.2 0.0 copy-done.1
  22.2 0.0 copy-done
  22.2 3.6 %shard_map.111.refs_1_ = f32[8,2,16,8,128]{4,3,2,1,0:T(8,128)S(1)} custom-call(f32[4,4,4096]{2,1,0:T(4,128)S(1)} %pad_maximum_fusion.refs_0_, f32[4,4,4096]{2,1,0:T(4,128)S(1)} %collective-permute-done.4.refs_1_, f32[4,4,4096]{2,1,0:T(4,128)S(1)} %collective-permute-done.5.refs_2_, f32[4,4,4096]{2,1,0:T(4,128)S(1)} %collective-permute-done.6.refs_3_, ...), custom_call_target="tpu_custom_call" | custom-call | tf_op jit(solution)/shard_map/pallas_call | solution.py:457
  25.8 2.0 %collective-permute-done.8.refs_0_ = f32[3,4,4096]{2,1,0:T(4,128)S(1)} collective-permute-done((f32[3,4,4096]{2,1,0:T(4,128)S(1)}, f32[3,4,4096]{2,1,0:T(4,128)S(1)}, u32[]{:S(2)}, u32[]{:S(2)}) %collective-permute-start.8) | collective-permute-done | bytes 196640 | tf_op jit(solution)/shard_map/ppermute | solution.py:495
  27.8 0.0 copy-start.3
  27.8 0.0 collective-permute-start.10
  27.8 0.0 collective-permute-done.9.refs_2_
  27.8 1.4 %collective-permute-done.10.refs_3_ = f32[3,4,4096]{2,1,0:T(4,128)S(1)} collective-permute-done((f32[3,4,4096]{2,1,0:T(4,128)S(1)}, f32[3,4,4096]{2,1,0:T(4,128)S(1)}, u32[]{:S(2)}, u32[]{:S(2)}) %collective-permute-start.10) | collective-permute-done | bytes 196640 | tf_op jit(solution)/shard_map/ppermute | solution.py:495
  29.2 2.9 %shard_map.113 = f32[8,2,12,8,128]{4,3,2,1,0:T(8,128)S(1)} custom-call(f32[3,4,4096]{2,1,0:T(4,128)S(1)} %collective-permute-done.7.refs_0_, f32[3,4,4096]{2,1,0:T(4,128)S(1)} %shard_map.112.refs_1_, f32[3,4,4096]{2,1,0:T(4,128)S(1)} %collective-permute-done.9.refs_2_, f32[3,4,4096]{2,1,0:T(4,128)S(1)} %collective-permute-done.10.refs_3_, ...), custom_call_target="tpu_custom_call" | custom-call | tf_op jit(solution)/shard_map/pallas_call | solution.py:457
  32.1 0.0 copy-done.3
  32.1 0.0 copy-start.2
  32.1 2.9 %shard_map.114 = f32[256,128]{1,0:T(8,128)S(1)} custom-call(f32[1,8,2,4,8,128]{5,4,3,2,1,0:T(8,128)S(1)} %bitcast.12, f32[1,8,2,16,8,128]{5,4,3,2,1,0:T(8,128)S(1)} %bitcast.10, f32[1,8,2,12,8,128]{5,4,3,2,1,0:T(8,128)S(1)} %bitcast.11, bf16[768,128]{1,0:T(8,128)(2,1)S(1)} %copy-done.3), custom_call_target="tpu_custom_call" | custom-call | tf_op jit(solution)/shard_map/pallas_call | solution.py:457
  35.0 0.0 copy-start.4
  35.0 0.0 copy-start.5
  35.0 11.3 %all_to_all.11 = f32[32,8,128]{2,1,0:T(8,128)S(1)} all-to-all(f32[32,8,128]{2,1,0:T(8,128)S(1)} %bitcast.15), channel_id=1, replica_groups=mesh['comp'=8,'rank'=4] {'comp','rank'}, dimensions={0} | all-to-all | bytes 262144 | tf_op jit(solution)/shard_map/all_to_all | solution.py:595
  46.3 0.0 copy-done.2
  46.3 0.0 copy-done.4
  46.3 0.0 copy-done.5
  46.3 0.9 %shard_map.115 = f32[128,128]{1,0:T(8,128)} custom-call(f32[256,128]{1,0:T(8,128)S(1)} %bitcast.16, f32[256,128]{1,0:T(8,128)S(1)} %copy-done.4, f32[256,128]{1,0:T(8,128)S(1)} %copy-done.5, bf16[128,1536]{1,0:T(8,128)(2,1)S(1)} %copy-done.2), custom_call_target="tpu_custom_call" | custom-call | tf_op jit(solution)/shard_map/pallas_call | solution.py:457
  (3 shorter events, 0.0 us)
Async XLA Ops:
  0.0 10.3 %copy-start.6 = (f32[8,32]{1,0:T(8,128)S(1)}, f32[8,32]{1,0:T(8,128)}, u32[]{:S(2)}) copy-start(f32[8,32]{1,0:T(8,128)} %refs_6_.5) | copy-start | bytes 3076
  0.0 10.3 %copy-start.7 = (f32[8,32]{1,0:T(8,128)S(1)}, f32[8,32]{1,0:T(8,128)}, u32[]{:S(2)}) copy-start(f32[8,32]{1,0:T(8,128)} %refs_7_.3) | copy-start | bytes 3076
  0.9 12.4 %collective-permute-start.2 = (f32[4,4096]{1,0:T(4,128)S(1)}, f32[4,4096]{1,0:T(4,128)S(1)}, u32[]{:S(2)}, u32[]{:S(2)}) collective-permute-start(f32[4,4096]{1,0:T(4,128)S(1)} %constant_dynamic-slice_fusion), channel_id=1, source_target_pairs={{0,16},{4,20},{8,24},{12,28},{16,0},{20,4},{24,8},{28,12},{1,17},{... | collective-permute-start | bytes 196616 | tf_op jit(solution)/shard_map/ppermute | solution.py:489
  4.9 8.5 %collective-permute-start.1 = (f32[4,4096]{1,0:T(4,128)S(1)}, f32[4,4096]{1,0:T(4,128)S(1)}, u32[]{:S(2)}, u32[]{:S(2)}) collective-permute-start(f32[4,4096]{1,0:T(4,128)S(1)} %constant_dynamic-slice_fusion), channel_id=1, source_target_pairs={{0,8},{4,12},{8,16},{12,20},{16,24},{20,28},{24,0},{28,4},{1,9},{5... | collective-permute-start | bytes 196616 | tf_op jit(solution)/shard_map/ppermute | solution.py:489
  6.5 6.9 %collective-permute-start.3 = (f32[4,4096]{1,0:T(4,128)S(1)}, f32[4,4096]{1,0:T(4,128)S(1)}, u32[]{:S(2)}, u32[]{:S(2)}) collective-permute-start(f32[4,4096]{1,0:T(4,128)S(1)} %constant_dynamic-slice_fusion), channel_id=1, source_target_pairs={{0,24},{4,28},{8,0},{12,4},{16,8},{20,12},{24,16},{28,20},{1,25},{... | collective-permute-start | bytes 196616 | tf_op jit(solution)/shard_map/ppermute | solution.py:489
  8.7 4.7 %collective-permute-start = (f32[4,4096]{1,0:T(4,128)S(1)}, f32[4,4096]{1,0:T(4,128)S(1)}, u32[]{:S(2)}, u32[]{:S(2)}) collective-permute-start(f32[4,4096]{1,0:T(4,128)S(1)} %constant_dynamic-slice_fusion), channel_id=1, source_target_pairs={{0,4},{4,0},{8,12},{12,8},{16,20},{20,16},{24,28},{28,24},{1,5},{5... | collective-permute-start | bytes 196616 | tf_op jit(solution)/shard_map/ppermute | solution.py:492
  13.3 8.9 %copy-start.1 = (f32[8,16384]{1,0:T(8,128)S(1)}, f32[8,16384]{1,0:T(8,128)}, u32[]{:S(2)}) copy-start(f32[8,16384]{1,0:T(8,128)} %refs_5_.5) | copy-start | bytes 1572868
  13.4 8.8 %copy-start = (f32[8,16384]{1,0:T(8,128)S(1)}, f32[8,16384]{1,0:T(8,128)}, u32[]{:S(2)}) copy-start(f32[8,16384]{1,0:T(8,128)} %refs_4_.5) | copy-start | bytes 1572868
  13.5 7.0 %collective-permute-start.4 = (f32[4,4,4096]{2,1,0:T(4,128)S(1)}, f32[4,4,4096]{2,1,0:T(4,128)S(1)}, u32[]{:S(2)}, u32[]{:S(2)}) collective-permute-start(f32[4,4,4096]{2,1,0:T(4,128)S(1)} %pad_maximum_fusion.refs_0_), channel_id=1, source_target_pairs={{0,2},{1,3},{2,0},{3,1},{4,6},{5,7},{6,4},{7,5},{8,10},{9,11},{10,... | collective-permute-start | bytes 786440 | tf_op jit(solution)/shard_map/ppermute | solution.py:495
  15.1 5.7 %collective-permute-start.7 = (f32[3,4,4096]{2,1,0:T(4,128)S(1)}, f32[3,4,4096]{2,1,0:T(4,128)S(1)}, u32[]{:S(2)}, u32[]{:S(2)}) collective-permute-start(f32[3,4,4096]{2,1,0:T(4,128)S(1)} %pad_maximum_fusion.1), channel_id=1, source_target_pairs={{0,4},{4,0},{8,12},{12,8},{16,20},{20,16},{24,28},{28,24},{1,5},{5... | collective-permute-start | bytes 589832 | tf_op jit(solution)/shard_map/ppermute | solution.py:492
  16.3 5.9 %collective-permute-start.5 = (f32[4,4,4096]{2,1,0:T(4,128)S(1)}, f32[4,4,4096]{2,1,0:T(4,128)S(1)}, u32[]{:S(2)}, u32[]{:S(2)}) collective-permute-start(f32[4,4,4096]{2,1,0:T(4,128)S(1)} %pad_maximum_fusion.refs_0_), channel_id=1, source_target_pairs={{0,1},{1,0},{2,3},{3,2},{4,5},{5,4},{6,7},{7,6},{8,9},{9,8},{10,11... | collective-permute-start | bytes 786440 | tf_op jit(solution)/shard_map/ppermute | solution.py:495
  20.5 1.7 %collective-permute-start.6 = (f32[4,4,4096]{2,1,0:T(4,128)S(1)}, f32[4,4,4096]{2,1,0:T(4,128)S(1)}, u32[]{:S(2)}, u32[]{:S(2)}) collective-permute-start(f32[4,4,4096]{2,1,0:T(4,128)S(1)} %collective-permute-done.4.refs_1_), channel_id=1, source_target_pairs={{0,1},{1,0},{2,3},{3,2},{4,5},{5,4},{6,7},{7,6},{8,9},{9,8},{10,11... | collective-permute-start | bytes 786440 | tf_op jit(solution)/shard_map/ppermute | solution.py:495
  20.8 7.0 %collective-permute-start.8 = (f32[3,4,4096]{2,1,0:T(4,128)S(1)}, f32[3,4,4096]{2,1,0:T(4,128)S(1)}, u32[]{:S(2)}, u32[]{:S(2)}) collective-permute-start(f32[3,4,4096]{2,1,0:T(4,128)S(1)} %collective-permute-done.7.refs_0_), channel_id=1, source_target_pairs={{0,2},{1,3},{2,0},{3,1},{4,6},{5,7},{6,4},{7,5},{8,10},{9,11},{10,... | collective-permute-start | bytes 589832 | tf_op jit(solution)/shard_map/ppermute | solution.py:495
  22.0 5.8 %collective-permute-start.9 = (f32[3,4,4096]{2,1,0:T(4,128)S(1)}, f32[3,4,4096]{2,1,0:T(4,128)S(1)}, u32[]{:S(2)}, u32[]{:S(2)}) collective-permute-start(f32[3,4,4096]{2,1,0:T(4,128)S(1)} %collective-permute-done.7.refs_0_), channel_id=1, source_target_pairs={{0,1},{1,0},{2,3},{3,2},{4,5},{5,4},{6,7},{7,6},{8,9},{9,8},{10,11... | collective-permute-start | bytes 589832 | tf_op jit(solution)/shard_map/ppermute | solution.py:495
  27.8 4.3 %copy-start.3 = (bf16[768,128]{1,0:T(8,128)(2,1)S(1)}, bf16[768,128]{1,0:T(8,128)(2,1)}, u32[]{:S(2)}) copy-start(bf16[768,128]{1,0:T(8,128)(2,1)} %constant.38.refs_3_) | copy-start | bytes 589828
  27.8 1.4 %collective-permute-start.10 = (f32[3,4,4096]{2,1,0:T(4,128)S(1)}, f32[3,4,4096]{2,1,0:T(4,128)S(1)}, u32[]{:S(2)}, u32[]{:S(2)}) collective-permute-start(f32[3,4,4096]{2,1,0:T(4,128)S(1)} %shard_map.112.refs_1_), channel_id=1, source_target_pairs={{0,1},{1,0},{2,3},{3,2},{4,5},{5,4},{6,7},{7,6},{8,9},{9,8},{10,11... | collective-permute-start | bytes 589832 | tf_op jit(solution)/shard_map/ppermute | solution.py:495
  32.1 14.2 %copy-start.2 = (bf16[128,1536]{1,0:T(8,128)(2,1)S(1)}, bf16[128,1536]{1,0:T(8,128)(2,1)}, u32[]{:S(2)}) copy-start(bf16[128,1536]{1,0:T(8,128)(2,1)} %constant.43.refs_3_) | copy-start | bytes 1179652
  35.0 11.3 %copy-start.4 = (f32[256,128]{1,0:T(8,128)S(1)}, f32[256,128]{1,0:T(8,128)}, u32[]{:S(2)}) copy-start(f32[256,128]{1,0:T(8,128)} %constant.25.clone.refs_1_) | copy-start | bytes 393220
  35.0 11.3 %copy-start.5 = (f32[256,128]{1,0:T(8,128)S(1)}, f32[256,128]{1,0:T(8,128)}, u32[]{:S(2)}) copy-start(f32[256,128]{1,0:T(8,128)} %constant.26.clone.refs_2_) | copy-start | bytes 393220

commit v4 on v3

--- a/solution.py
+++ b/solution.py
@@ -525,10 +525,14 @@
     near = jnp.stack([flipped_own, *lined])
     flipped = across(jnp.stack(lined))
     beyond = swapped(near, 2)
-    ready = [near, beyond, swapped(near, 1), swapped(beyond, 1)]
+    beside = swapped(jnp.concatenate([near, beyond]), 1)
+    count = len(early)
+    joined = [
+        (((0, k), (1, k), (2, k), (2, count + k)), *place) for k, place in enumerate(early)
+    ]
     flipped_beyond = swapped(flipped, 2)
     flipped_beside = swapped(flipped, 1)
-    first = joined_spectra(ready, quartered(early))
+    first = joined_spectra([near, beyond, beside], joined)
     (flipped_beyond,) = after([flipped_beyond], first)
     second = joined_spectra(
         [flipped, flipped_beyond, flipped_beside, swapped(flipped_beyond, 1)], quartered(late)

time: 47.4 us -> 54.2 us (1.14)
  waiting for transfers between devices: 7.96 us -> 14.9 us
    ppermute x2, waiting for transfers between devices: 0.35 us -> 6.71 us  [across(): return lax.ppermute(block, 'comp', [(c, c ^ 1) for c in range(comps)])]
    ppermute x6 -> x5, waiting for transfers between devices: 7.6 us -> 8.18 us  [swapped(): return lax.ppermute(block, 'rank', [(r, r ^ other) for r in range(ranks)])]
    ppermute x6 -> x5, starting transfers between devices: 2.94 us -> 3.12 us  [swapped(): return lax.ppermute(block, 'rank', [(r, r ^ other) for r in range(ranks)])]
  transfers between devices with their start and end apart: 11 -> 10, of which waited for: 4 -> 4; matrix products, arithmetic and copies ran while one was open for 0% -> 0% of each run, Pallas kernels for 14% -> 12%
where the time goes in v4:
time: 54.2 us; the launch traced here: 54 us
  waiting for transfers between devices  14.9 us (27%)
  Pallas kernels  13.3 us (25%)
  starting transfers between devices  13.2 us (24%)
  blocking collectives  11.3 us (21%)
  local copies, waits for them, and re-layouts  1 us (2%)
    pallas_call x5, Pallas kernels, whole_call(): pl.pallas_call(kernel, out_shape=[out_type(shape, jnp.float32) for shape...  13.3 us
    all_to_all x1, blocking collectives, body(): spread = lax.all_to_all(sent, AXES, split_axis=0, concat_axis=0, tiled=True)  11.3 us
    ppermute x5, waiting for transfers between devices, swapped(): return lax.ppermute(block, 'rank', [(r, r ^ other) for r in range(ranks)])  8.18 us
    ppermute x3, starting transfers between devices, along(): return lax.ppermute(block, 'comp', pairs)  7.86 us
    ppermute x2, waiting for transfers between devices, across(): return lax.ppermute(block, 'comp', [(c, c ^ 1) for c in range(comps)])  6.71 us
    ppermute x5, starting transfers between devices, swapped(): return lax.ppermute(block, 'rank', [(r, r ^ other) for r in range(ranks)])  3.12 us
    ppermute x2, starting transfers between devices, across(): return lax.ppermute(block, 'comp', [(c, c ^ 1) for c in range(comps)])  2.17 us
  transfers between devices with their start and end apart: 10, of which 4 were waited for; matrix products, arithmetic and copies ran while one was open for 0% of the time, Pallas kernels for 12%

profile of v4, /device:TPU:0, one launch (start us, length us, event | category | flops | bytes accessed | tf_op | source)
XLA Modules:
  0.0 54.0 jit_solution(5890783157318791433)
XLA Ops:
  0.0 0.0 copy-start.6
  0.0 0.0 copy-start.7
  0.0 0.9 %constant_dynamic-slice_fusion = f32[4,4096]{1,0:T(4,128)S(1)} fusion(f32[4,16384]{1,0:T(4,128)} %refs_4_.3, s32[]{:T(128)S(6)} %select_n.3), kind=kLoop, calls=%fused_computation.7 | loop fusion | bytes 131076 | tf_op jit(solution)/shard_map/dynamic_slice | solution.py:485
  0.9 4.0 %collective-permute-start.2 = (f32[4,4096]{1,0:T(4,128)S(1)}, f32[4,4096]{1,0:T(4,128)S(1)}, u32[]{:S(2)}, u32[]{:S(2)}) collective-permute-start(f32[4,4096]{1,0:T(4,128)S(1)} %constant_dynamic-slice_fusion), channel_id=1, source_target_pairs={{0,16},{4,20},{8,24},{12,28},{16,0},{20,4},{24,8},{28,12},{1,17},{... | collective-permute-start | bytes 196616 | tf_op jit(solution)/shard_map/ppermute | solution.py:489
  4.9 1.6 %collective-permute-start.1 = (f32[4,4096]{1,0:T(4,128)S(1)}, f32[4,4096]{1,0:T(4,128)S(1)}, u32[]{:S(2)}, u32[]{:S(2)}) collective-permute-start(f32[4,4096]{1,0:T(4,128)S(1)} %constant_dynamic-slice_fusion), channel_id=1, source_target_pairs={{0,8},{4,12},{8,16},{12,20},{16,24},{20,28},{24,0},{28,4},{1,9},{5... | collective-permute-start | bytes 196616 | tf_op jit(solution)/shard_map/ppermute | solution.py:489
  6.5 2.2 %collective-permute-start.3 = (f32[4,4096]{1,0:T(4,128)S(1)}, f32[4,4096]{1,0:T(4,128)S(1)}, u32[]{:S(2)}, u32[]{:S(2)}) collective-permute-start(f32[4,4096]{1,0:T(4,128)S(1)} %constant_dynamic-slice_fusion), channel_id=1, source_target_pairs={{0,24},{4,28},{8,0},{12,4},{16,8},{20,12},{24,16},{28,20},{1,25},{... | collective-permute-start | bytes 196616 | tf_op jit(solution)/shard_map/ppermute | solution.py:489
  8.7 1.5 %collective-permute-start = (f32[4,4096]{1,0:T(4,128)S(1)}, f32[4,4096]{1,0:T(4,128)S(1)}, u32[]{:S(2)}, u32[]{:S(2)}) collective-permute-start(f32[4,4096]{1,0:T(4,128)S(1)} %constant_dynamic-slice_fusion), channel_id=1, source_target_pairs={{0,4},{4,0},{8,12},{12,8},{16,20},{20,16},{24,28},{28,24},{1,5},{5... | collective-permute-start | bytes 196616 | tf_op jit(solution)/shard_map/ppermute | solution.py:492
  10.3 0.0 copy-done.6
  10.3 0.0 copy-done.7
  10.3 3.1 %shard_map.109.refs_1_ = f32[8,2,4,8,128]{4,3,2,1,0:T(8,128)S(1)} custom-call(f32[8,32]{1,0:T(8,128)S(1)} %copy-done.6, f32[8,32]{1,0:T(8,128)S(1)} %copy-done.7, f32[4,2,8,128]{3,2,1,0:T(8,128)} %constant.22.clone.refs_2_.refs_7_.refs_8_, bf16[768,256]{1,0:T(8,128)(2,1)} %constant.33.refs_3_.refs_8_.refs_9_, f32[4,16384]{1,0:T(4,128)} %refs_4_.3, ...), custom_call_target="tpu_custom_call" | custom-call | tf_op jit(solution)/shard_map/pallas_call | solution.py:457
  13.3 0.0 collective-permute-done.2.refs_0_
  13.3 0.0 collective-permute-done.1
  13.4 0.0 collective-permute-done.3
  13.4 0.0 collective-permute-done
  13.4 0.1 pad_maximum_fusion.refs_0_
  13.4 1.6 %collective-permute-start.4 = (f32[4,4,4096]{2,1,0:T(4,128)S(1)}, f32[4,4,4096]{2,1,0:T(4,128)S(1)}, u32[]{:S(2)}, u32[]{:S(2)}) collective-permute-start(f32[4,4,4096]{2,1,0:T(4,128)S(1)} %pad_maximum_fusion.refs_0_), channel_id=1, source_target_pairs={{0,2},{1,3},{2,0},{3,1},{4,6},{5,7},{6,4},{7,5},{8,10},{9,11},{10,... | collective-permute-start | bytes 786440 | tf_op jit(solution)/shard_map/ppermute | solution.py:495
  15.0 0.0 copy-start.1
  15.1 0.0 copy-start
  15.1 5.4 %collective-permute-done.4.refs_1_ = f32[4,4,4096]{2,1,0:T(4,128)S(1)} collective-permute-done((f32[4,4,4096]{2,1,0:T(4,128)S(1)}, f32[4,4,4096]{2,1,0:T(4,128)S(1)}, u32[]{:S(2)}, u32[]{:S(2)}) %collective-permute-start.4) | collective-permute-done | bytes 262176 | tf_op jit(solution)/shard_map/ppermute | solution.py:495
  20.5 0.1 collective-permute-start.5
  20.6 0.7 %collective-permute-start.6 = (f32[3,4,4096]{2,1,0:T(4,128)S(1)}, f32[3,4,4096]{2,1,0:T(4,128)S(1)}, u32[]{:S(2)}, u32[]{:S(2)}) collective-permute-start(f32[3,4,4096]{2,1,0:T(4,128)S(1)} %pad_maximum_fusion.1), channel_id=1, source_target_pairs={{0,4},{4,0},{8,12},{12,8},{16,20},{20,16},{24,28},{28,24},{1,5},{5... | collective-permute-start | bytes 589832 | tf_op jit(solution)/shard_map/ppermute | solution.py:492
  21.3 6.7 %collective-permute-done.6.refs_0_ = f32[3,4,4096]{2,1,0:T(4,128)S(1)} collective-permute-done((f32[3,4,4096]{2,1,0:T(4,128)S(1)}, f32[3,4,4096]{2,1,0:T(4,128)S(1)}, u32[]{:S(2)}, u32[]{:S(2)}) %collective-permute-start.6) | collective-permute-done | bytes 196640 | tf_op jit(solution)/shard_map/ppermute | solution.py:492
  28.0 1.5 %collective-permute-start.7 = (f32[3,4,4096]{2,1,0:T(4,128)S(1)}, f32[3,4,4096]{2,1,0:T(4,128)S(1)}, u32[]{:S(2)}, u32[]{:S(2)}) collective-permute-start(f32[3,4,4096]{2,1,0:T(4,128)S(1)} %collective-permute-done.6.refs_0_), channel_id=1, source_target_pairs={{0,2},{1,3},{2,0},{3,1},{4,6},{5,7},{6,4},{7,5},{8,10},{9,11},{10,... | collective-permute-start | bytes 589832 | tf_op jit(solution)/shard_map/ppermute | solution.py:495
  29.5 0.0 collective-permute-start.8
  29.5 0.0 collective-permute-done.5.refs_2_
  29.5 0.0 copy-done.1
  29.5 0.0 copy-done
  29.5 3.6 %shard_map.111.refs_1_ = f32[8,2,16,8,128]{4,3,2,1,0:T(8,128)S(1)} custom-call(f32[4,4,4096]{2,1,0:T(4,128)S(1)} %pad_maximum_fusion.refs_0_, f32[4,4,4096]{2,1,0:T(4,128)S(1)} %collective-permute-done.4.refs_1_, f32[8,4,4096]{2,1,0:T(4,128)S(1)} %collective-permute-done.5.refs_2_, f32[8,16384]{1,0:T(8,128)S(1)} %copy-done, f32[8,16384]{1,0:T(8,128)S(1)} %copy-done.1, ...), custom_call_target="tpu_custom_call" | custom-call | tf_op jit(solution)/shard_map/pallas_call | solution.py:457
  33.1 1.4 %collective-permute-done.7.refs_0_ = f32[3,4,4096]{2,1,0:T(4,128)S(1)} collective-permute-done((f32[3,4,4096]{2,1,0:T(4,128)S(1)}, f32[3,4,4096]{2,1,0:T(4,128)S(1)}, u32[]{:S(2)}, u32[]{:S(2)}) %collective-permute-start.7) | collective-permute-done | bytes 196640 | tf_op jit(solution)/shard_map/ppermute | solution.py:495
  34.5 0.0 copy-start.3
  34.5 0.0 collective-permute-start.9
  34.5 0.0 collective-permute-done.8.refs_2_
  34.5 1.4 %collective-permute-done.9.refs_3_ = f32[3,4,4096]{2,1,0:T(4,128)S(1)} collective-permute-done((f32[3,4,4096]{2,1,0:T(4,128)S(1)}, f32[3,4,4096]{2,1,0:T(4,128)S(1)}, u32[]{:S(2)}, u32[]{:S(2)}) %collective-permute-start.9) | collective-permute-done | bytes 196640 | tf_op jit(solution)/shard_map/ppermute | solution.py:495
  35.9 2.9 %shard_map.113 = f32[8,2,12,8,128]{4,3,2,1,0:T(8,128)S(1)} custom-call(f32[3,4,4096]{2,1,0:T(4,128)S(1)} %collective-permute-done.6.refs_0_, f32[3,4,4096]{2,1,0:T(4,128)S(1)} %shard_map.112.refs_1_, f32[3,4,4096]{2,1,0:T(4,128)S(1)} %collective-permute-done.8.refs_2_, f32[3,4,4096]{2,1,0:T(4,128)S(1)} %collective-permute-done.9.refs_3_, ...), custom_call_target="tpu_custom_call" | custom-call | tf_op jit(solution)/shard_map/pallas_call | solution.py:457
  38.8 0.0 copy-done.3
  38.8 0.0 copy-start.2
  38.8 2.9 %shard_map.114 = f32[256,128]{1,0:T(8,128)S(1)} custom-call(f32[1,8,2,4,8,128]{5,4,3,2,1,0:T(8,128)S(1)} %bitcast.16, f32[1,8,2,16,8,128]{5,4,3,2,1,0:T(8,128)S(1)} %bitcast.14, f32[1,8,2,12,8,128]{5,4,3,2,1,0:T(8,128)S(1)} %bitcast.15, bf16[768,128]{1,0:T(8,128)(2,1)S(1)} %copy-done.3), custom_call_target="tpu_custom_call" | custom-call | tf_op jit(solution)/shard_map/pallas_call | solution.py:457
  41.7 0.0 copy-start.4
  41.7 0.0 copy-start.5
  41.7 11.3 %all_to_all.11 = f32[32,8,128]{2,1,0:T(8,128)S(1)} all-to-all(f32[32,8,128]{2,1,0:T(8,128)S(1)} %bitcast.19), channel_id=1, replica_groups=mesh['comp'=8,'rank'=4] {'comp','rank'}, dimensions={0} | all-to-all | bytes 262144 | tf_op jit(solution)/shard_map/all_to_all | solution.py:599
  53.0 0.0 copy-done.2
  53.0 0.0 copy-done.4
  53.1 0.0 copy-done.5
  53.1 0.9 %shard_map.115 = f32[128,128]{1,0:T(8,128)} custom-call(f32[256,128]{1,0:T(8,128)S(1)} %bitcast.20, f32[256,128]{1,0:T(8,128)S(1)} %copy-done.4, f32[256,128]{1,0:T(8,128)S(1)} %copy-done.5, bf16[128,1536]{1,0:T(8,128)(2,1)S(1)} %copy-done.2), custom_call_target="tpu_custom_call" | custom-call | tf_op jit(solution)/shard_map/pallas_call | solution.py:457
  (8 shorter events, 0.1 us)
Async XLA Ops:
  0.0 10.3 %copy-start.6 = (f32[8,32]{1,0:T(8,128)S(1)}, f32[8,32]{1,0:T(8,128)}, u32[]{:S(2)}) copy-start(f32[8,32]{1,0:T(8,128)} %refs_6_.5) | copy-start | bytes 3076
  0.0 10.3 %copy-start.7 = (f32[8,32]{1,0:T(8,128)S(1)}, f32[8,32]{1,0:T(8,128)}, u32[]{:S(2)}) copy-start(f32[8,32]{1,0:T(8,128)} %refs_7_.2) | copy-start | bytes 3076
  0.9 12.4 %collective-permute-start.2 = (f32[4,4096]{1,0:T(4,128)S(1)}, f32[4,4096]{1,0:T(4,128)S(1)}, u32[]{:S(2)}, u32[]{:S(2)}) collective-permute-start(f32[4,4096]{1,0:T(4,128)S(1)} %constant_dynamic-slice_fusion), channel_id=1, source_target_pairs={{0,16},{4,20},{8,24},{12,28},{16,0},{20,4},{24,8},{28,12},{1,17},{... | collective-permute-start | bytes 196616 | tf_op jit(solution)/shard_map/ppermute | solution.py:489
  4.9 8.4 %collective-permute-start.1 = (f32[4,4096]{1,0:T(4,128)S(1)}, f32[4,4096]{1,0:T(4,128)S(1)}, u32[]{:S(2)}, u32[]{:S(2)}) collective-permute-start(f32[4,4096]{1,0:T(4,128)S(1)} %constant_dynamic-slice_fusion), channel_id=1, source_target_pairs={{0,8},{4,12},{8,16},{12,20},{16,24},{20,28},{24,0},{28,4},{1,9},{5... | collective-permute-start | bytes 196616 | tf_op jit(solution)/shard_map/ppermute | solution.py:489
  6.5 6.9 %collective-permute-start.3 = (f32[4,4096]{1,0:T(4,128)S(1)}, f32[4,4096]{1,0:T(4,128)S(1)}, u32[]{:S(2)}, u32[]{:S(2)}) collective-permute-start(f32[4,4096]{1,0:T(4,128)S(1)} %constant_dynamic-slice_fusion), channel_id=1, source_target_pairs={{0,24},{4,28},{8,0},{12,4},{16,8},{20,12},{24,16},{28,20},{1,25},{... | collective-permute-start | bytes 196616 | tf_op jit(solution)/shard_map/ppermute | solution.py:489
  8.7 4.6 %collective-permute-start = (f32[4,4096]{1,0:T(4,128)S(1)}, f32[4,4096]{1,0:T(4,128)S(1)}, u32[]{:S(2)}, u32[]{:S(2)}) collective-permute-start(f32[4,4096]{1,0:T(4,128)S(1)} %constant_dynamic-slice_fusion), channel_id=1, source_target_pairs={{0,4},{4,0},{8,12},{12,8},{16,20},{20,16},{24,28},{28,24},{1,5},{5... | collective-permute-start | bytes 196616 | tf_op jit(solution)/shard_map/ppermute | solution.py:492
  13.4 7.0 %collective-permute-start.4 = (f32[4,4,4096]{2,1,0:T(4,128)S(1)}, f32[4,4,4096]{2,1,0:T(4,128)S(1)}, u32[]{:S(2)}, u32[]{:S(2)}) collective-permute-start(f32[4,4,4096]{2,1,0:T(4,128)S(1)} %pad_maximum_fusion.refs_0_), channel_id=1, source_target_pairs={{0,2},{1,3},{2,0},{3,1},{4,6},{5,7},{6,4},{7,5},{8,10},{9,11},{10,... | collective-permute-start | bytes 786440 | tf_op jit(solution)/shard_map/ppermute | solution.py:495
  15.0 14.5 %copy-start.1 = (f32[8,16384]{1,0:T(8,128)S(1)}, f32[8,16384]{1,0:T(8,128)}, u32[]{:S(2)}) copy-start(f32[8,16384]{1,0:T(8,128)} %refs_5_.5) | copy-start | bytes 1572868
  15.1 14.4 %copy-start = (f32[8,16384]{1,0:T(8,128)S(1)}, f32[8,16384]{1,0:T(8,128)}, u32[]{:S(2)}) copy-start(f32[8,16384]{1,0:T(8,128)} %refs_4_.5) | copy-start | bytes 1572868
  20.5 9.0 %collective-permute-start.5 = (f32[8,4,4096]{2,1,0:T(4,128)S(1)}, f32[8,4,4096]{2,1,0:T(4,128)S(1)}, u32[]{:S(2)}, u32[]{:S(2)}) collective-permute-start(f32[8,4,4096]{2,1,0:T(4,128)S(1)} %constant_dynamic-update-slice_fusion), channel_id=1, source_target_pairs={{0,1},{1,0},{2,3},{3,2},{4,5},{5,4},{6,7},{7,6},{8,9},{9,8},{10,11... | collective-permute-start | bytes 1572872 | tf_op jit(solution)/shard_map/ppermute | solution.py:495
  20.6 7.4 %collective-permute-start.6 = (f32[3,4,4096]{2,1,0:T(4,128)S(1)}, f32[3,4,4096]{2,1,0:T(4,128)S(1)}, u32[]{:S(2)}, u32[]{:S(2)}) collective-permute-start(f32[3,4,4096]{2,1,0:T(4,128)S(1)} %pad_maximum_fusion.1), channel_id=1, source_target_pairs={{0,4},{4,0},{8,12},{12,8},{16,20},{20,16},{24,28},{28,24},{1,5},{5... | collective-permute-start | bytes 589832 | tf_op jit(solution)/shard_map/ppermute | solution.py:492
  28.0 6.5 %collective-permute-start.7 = (f32[3,4,4096]{2,1,0:T(4,128)S(1)}, f32[3,4,4096]{2,1,0:T(4,128)S(1)}, u32[]{:S(2)}, u32[]{:S(2)}) collective-permute-start(f32[3,4,4096]{2,1,0:T(4,128)S(1)} %collective-permute-done.6.refs_0_), channel_id=1, source_target_pairs={{0,2},{1,3},{2,0},{3,1},{4,6},{5,7},{6,4},{7,5},{8,10},{9,11},{10,... | collective-permute-start | bytes 589832 | tf_op jit(solution)/shard_map/ppermute | solution.py:495
  29.5 5.0 %collective-permute-start.8 = (f32[3,4,4096]{2,1,0:T(4,128)S(1)}, f32[3,4,4096]{2,1,0:T(4,128)S(1)}, u32[]{:S(2)}, u32[]{:S(2)}) collective-permute-start(f32[3,4,4096]{2,1,0:T(4,128)S(1)} %collective-permute-done.6.refs_0_), channel_id=1, source_target_pairs={{0,1},{1,0},{2,3},{3,2},{4,5},{5,4},{6,7},{7,6},{8,9},{9,8},{10,11... | collective-permute-start | bytes 589832 | tf_op jit(solution)/shard_map/ppermute | solution.py:495
  34.5 4.3 %copy-start.3 = (bf16[768,128]{1,0:T(8,128)(2,1)S(1)}, bf16[768,128]{1,0:T(8,128)(2,1)}, u32[]{:S(2)}) copy-start(bf16[768,128]{1,0:T(8,128)(2,1)} %constant.38.refs_3_) | copy-start | bytes 589828
  34.5 1.4 %collective-permute-start.9 = (f32[3,4,4096]{2,1,0:T(4,128)S(1)}, f32[3,4,4096]{2,1,0:T(4,128)S(1)}, u32[]{:S(2)}, u32[]{:S(2)}) collective-permute-start(f32[3,4,4096]{2,1,0:T(4,128)S(1)} %shard_map.112.refs_1_), channel_id=1, source_target_pairs={{0,1},{1,0},{2,3},{3,2},{4,5},{5,4},{6,7},{7,6},{8,9},{9,8},{10,11... | collective-permute-start | bytes 589832 | tf_op jit(solution)/shard_map/ppermute | solution.py:495
  38.8 14.2 %copy-start.2 = (bf16[128,1536]{1,0:T(8,128)(2,1)S(1)}, bf16[128,1536]{1,0:T(8,128)(2,1)}, u32[]{:S(2)}) copy-start(bf16[128,1536]{1,0:T(8,128)(2,1)} %constant.43.refs_3_) | copy-start | bytes 1179652
  41.7 11.4 %copy-start.4 = (f32[256,128]{1,0:T(8,128)S(1)}, f32[256,128]{1,0:T(8,128)}, u32[]{:S(2)}) copy-start(f32[256,128]{1,0:T(8,128)} %constant.25.clone.refs_1_) | copy-start | bytes 393220
  41.7 11.3 %copy-start.5 = (f32[256,128]{1,0:T(8,128)S(1)}, f32[256,128]{1,0:T(8,128)}, u32[]{:S(2)}) copy-start(f32[256,128]{1,0:T(8,128)} %constant.26.clone.refs_2_) | copy-start | bytes 393220
